TPU v7x, 128 devices: a whole 4x4x4 slice. The times are simulated.
128 devices in a mesh: ctx: 16 (over y, z_lo, core), head: 8 (over x, z_hi).
Axes of the slice: x: 4, y: 4, z: 4 (z_hi: 2, z_lo: 2; z = z_hi * 2 + z_lo), core: 2. Of those that a mesh axis runs over, the one named last changes fastest.
Arguments:
- activations: bfloat16 [6144, 4096], P('ctx'), may hold values from -24 to 24
- noise_mask: int32 [6144], P('ctx'), may hold values 0 or 1
- span_order: int32 [32], replicated, may hold values from 0 to 31, each once
- mask_vector: bfloat16 [4096], replicated, may hold values from -6 to 6
- input_weights: bfloat16 [3, 4096, 4096], P(None, None, 'head'), may hold values from -0.09375 to 0.09375
- output_weight: bfloat16 [4096, 4096], P('head'), may hold values from -0.09375 to 0.09375
Outputs:
- mixed_out: bfloat16 [6144, 8192], P(('ctx', 'head'))
Inputs may be any that keep to these rules, and one draw needn't show every extreme that they name: A permutation; slot s holds document tokens span_order[s] * (192) onward. `noise_mask`: 1 marks a token of the noisy copy replaced by mask_vector.
All inputs are finite; a program needn't handle non-finite values. No bound on the sum of `noise_mask` on one device may be relied on, other than what follows from the above.
Results may differ from a plain program's by a relative error of at most 0.019.
Values may be sent and summed in bfloat16 or wider, within the bound.
A program may use at most 128 MiB of HBM per device.

v0:
```python
import math

import jax
import jax.numpy as jnp
from jax import lax
from jax.sharding import PartitionSpec as P

HEAD_SIZE = 128
DIFFUSION_TOKENS = 64


def shifted(value, axis, steps):
    count = lax.axis_size(axis)
    pairs = [(source, (source + steps) % count) for source in range(count)]
    return lax.ppermute(value, axis, pairs)


def shards(activations, noise_mask, span_order, mask_vector, input_weights, output_weight):
    row_count = activations.shape[0]
    half_rows = row_count // 2
    ctx_count = lax.axis_size("ctx")
    ctx_index = lax.axis_index("ctx")
    local_width = input_weights.shape[2]
    local_heads = local_width // HEAD_SIZE
    logit_scale_factor = 1.0 / math.sqrt(HEAD_SIZE)
    noisy_rows = jnp.where(noise_mask[:, None] == 1, mask_vector[None, :], activations)
    stacked = jnp.concatenate([activations, noisy_rows], axis=0)
    projected = jnp.einsum(
        "td,sdc->stc", stacked, input_weights, preferred_element_type=jnp.float32
    ).astype(jnp.bfloat16)
    queries = projected[0].reshape(2 * row_count, local_heads, HEAD_SIZE)
    slot_ids = jnp.arange(2 * ctx_count, dtype=jnp.int32)

    def span_lookup(slot):
        return jnp.sum(jnp.where(slot_ids == slot, span_order, 0))

    row_index = ctx_index * row_count + jnp.arange(row_count, dtype=jnp.int32)
    onehot = (row_index // half_rows)[:, None] == slot_ids[None, :]
    span_ids = jnp.sum(jnp.where(onehot, span_order[None, :], 0), axis=1)
    own_positions = span_ids * half_rows + row_index % half_rows
    query_block = jnp.concatenate([own_positions, own_positions]) // DIFFUSION_TOKENS
    query_noisy = jnp.concatenate([jnp.zeros((row_count,), bool), jnp.ones((row_count,), bool)])
    groups = row_count // DIFFUSION_TOKENS
    grouped_query_rows = queries[row_count:].reshape(
        groups, DIFFUSION_TOKENS, local_heads, HEAD_SIZE
    )
    grouped_key_rows = projected[1][row_count:].reshape(
        groups, DIFFUSION_TOKENS, local_heads, HEAD_SIZE
    )
    grouped_value_rows = projected[2][row_count:].reshape(
        groups, DIFFUSION_TOKENS, local_heads, HEAD_SIZE
    )
    group_scores = (
        jnp.einsum(
            "bqhd,bkhd->hbqk",
            grouped_query_rows,
            grouped_key_rows,
            preferred_element_type=jnp.float32,
        )
        * logit_scale_factor
    )
    group_max = group_scores.max(axis=-1)
    group_weights = jnp.exp(group_scores - group_max[..., None])
    group_sums = group_weights.sum(axis=-1)
    group_output = jnp.einsum(
        "hbqk,bkhd->hbqd",
        group_weights.astype(jnp.bfloat16),
        grouped_value_rows,
        preferred_element_type=jnp.float32,
    )
    row_max = jnp.concatenate(
        [
            jnp.full((local_heads, row_count), -1e30, jnp.float32),
            group_max.reshape(local_heads, row_count),
        ],
        axis=1,
    )
    row_sum = jnp.concatenate(
        [
            jnp.zeros((local_heads, row_count), jnp.float32),
            group_sums.reshape(local_heads, row_count),
        ],
        axis=1,
    )
    accumulated = jnp.concatenate(
        [
            jnp.zeros((local_heads, row_count, HEAD_SIZE), jnp.float32),
            group_output.reshape(local_heads, row_count, HEAD_SIZE),
        ],
        axis=1,
    )
    carried = (row_max, row_sum, accumulated)

    def attend(running, key_values, key_positions):
        key_rows = key_values[0].reshape(-1, local_heads, HEAD_SIZE)
        value_rows = key_values[1].reshape(-1, local_heads, HEAD_SIZE)
        key_block = key_positions // DIFFUSION_TOKENS
        allowed = jnp.where(
            query_noisy[:, None],
            key_block[None, :] < query_block[:, None],
            key_block[None, :] <= query_block[:, None],
        )
        scores = (
            jnp.einsum("qhd,khd->hqk", queries, key_rows, preferred_element_type=jnp.float32)
            * logit_scale_factor
        )
        scores = jnp.where(allowed[None], scores, jnp.float32(-1e30))
        old_max, old_sum, old_output = running
        new_max = jnp.maximum(old_max, scores.max(axis=-1))
        weights = jnp.where(allowed[None], jnp.exp(scores - new_max[..., None]), jnp.float32(0.0))
        factor = jnp.exp(old_max - new_max)
        new_sum = old_sum * factor + weights.sum(axis=-1)
        new_output = old_output * factor[..., None] + jnp.einsum(
            "hqk,khd->hqd",
            weights.astype(jnp.bfloat16),
            value_rows,
            preferred_element_type=jnp.float32,
        )
        return (new_max, new_sum, new_output)

    def visit_tile(running, key_values, key_positions):
        return attend(running, key_values, key_positions)

    clean_pair = jnp.stack([projected[1][:row_count], projected[2][:row_count]])

    def shard_terms(running, key_values, source):
        for half_index in range(2):
            block_rows = key_values[:, half_index * half_rows : (half_index + 1) * half_rows]
            key_positions = span_lookup(2 * source + half_index) * half_rows + jnp.arange(
                half_rows, dtype=jnp.int32
            )
            running = visit_tile(running, block_rows, key_positions)
        return running

    carried = shard_terms(carried, clean_pair, ctx_index)

    def cycle_turn(turn_index, loop_state):
        key_values, running = loop_state
        key_values = shifted(key_values, "ctx", 1)
        source = (ctx_index - turn_index) % ctx_count
        return (key_values, shard_terms(running, key_values, source))

    clean_pair, carried = lax.fori_loop(1, ctx_count, cycle_turn, (clean_pair, carried))
    row_max, row_sum, accumulated = carried
    attended = (
        (accumulated / row_sum[..., None])
        .transpose(1, 0, 2)
        .reshape(2 * row_count, local_width)
        .astype(jnp.bfloat16)
    )
    clean_proj = jnp.dot(attended[:row_count], output_weight, preferred_element_type=jnp.float32)
    noisy_proj = jnp.dot(attended[row_count:], output_weight, preferred_element_type=jnp.float32)
    summands = jnp.concatenate([clean_proj, noisy_proj], axis=1)
    mixed_out = lax.psum_scatter(
        summands.astype(jnp.bfloat16), "head", scatter_dimension=0, tiled=True
    )
    return mixed_out


def solution(mesh):
    in_specs = (P("ctx", None), P("ctx"), P(), P(), P(None, None, "head"), P("head", None))
    out_specs = P(("ctx", "head"), None)
    return jax.shard_map(shards, mesh=mesh, in_specs=in_specs, out_specs=out_specs, check_vma=False)
```

profile of v0, /device:TPU:0, one launch (start us, length us, event | category | flops | bytes accessed | tf_op | source)
XLA Modules:
  0.0 602.2 jit_solution(14524082099952988250)
XLA Ops:
  10.1 13.0 %convert_bitcast_fusion = bf16[3,768,512]{2,1,0:T(8,128)(2,1)S(1)} fusion(bf16[3,4096,512]{2,1,0:T(8,128)(2,1)} %param.12, bf16[384,4096]{1,0:T(8,128)(2,1)S(1)} %broadcast_select_fusion, bf16[384,4096]{1,0:T(8,128)(2,1)S(1)} %copy-done.4), kind=kOutput, calls=%fused_computation.64 | convolution fusion | flops 9677438976 | bytes 21233664 | tf_op jit(solution)/shard_map/td,sdc->stc/dot_general | solution.py:28
  44.6 439.2 %while.24 = (s32[]{:T(128)}, bf16[2,384,512]{2,1,0:T(8,128)(2,1)}, f32[4,768]{1,0:T(4,128)S(1)}, f32[4,768]{1,0:T(4,128)S(1)}, f32[4,768,128]{2,1,0:T(8,128)S(1)...) while((s32[]{:T(128)}, bf16[2,384,512]{2,1,0:T(8,128)(2,1)}, ...), condition=%wide.region_16.17_spmd.clone.clone, body=%wide.region_9.16_spmd.clone.clone.sunk | while | flops 621791424 | bytes 34536784 | solution.py:143
  47.2 11.4 %collective-permute-done = bf16[2,384,512]{2,1,0:T(8,128)(2,1)S(1)} collective-permute-done((bf16[2,384,512]{2,1,0:T(8,128)(2,1)}, bf16[2,384,512]{2,1,0:T(8,128)(2,1)S(1)}, u32[]{:S(2)}, u32[]{:S(2)}) %collective-permute-start) | collective-permute-done | bytes 786464 | tf_op jit(solution)/shard_map/while/body/eval_jaxpr/ppermute | solution.py:15
  70.9 2.4 multiply_add_fusion.7
  76.5 11.4 %collective-permute-done = bf16[2,384,512]{2,1,0:T(8,128)(2,1)S(1)} collective-permute-done((bf16[2,384,512]{2,1,0:T(8,128)(2,1)}, bf16[2,384,512]{2,1,0:T(8,128)(2,1)S(1)}, u32[]{:S(2)}, u32[]{:S(2)}) %collective-permute-start) | collective-permute-done | bytes 786464 | tf_op jit(solution)/shard_map/while/body/eval_jaxpr/ppermute | solution.py:15
  100.1 2.4 multiply_add_fusion.7
  105.8 11.4 %collective-permute-done = bf16[2,384,512]{2,1,0:T(8,128)(2,1)S(1)} collective-permute-done((bf16[2,384,512]{2,1,0:T(8,128)(2,1)}, bf16[2,384,512]{2,1,0:T(8,128)(2,1)S(1)}, u32[]{:S(2)}, u32[]{:S(2)}) %collective-permute-start) | collective-permute-done | bytes 786464 | tf_op jit(solution)/shard_map/while/body/eval_jaxpr/ppermute | solution.py:15
  129.4 2.4 multiply_add_fusion.7
  135.0 11.4 %collective-permute-done = bf16[2,384,512]{2,1,0:T(8,128)(2,1)S(1)} collective-permute-done((bf16[2,384,512]{2,1,0:T(8,128)(2,1)}, bf16[2,384,512]{2,1,0:T(8,128)(2,1)S(1)}, u32[]{:S(2)}, u32[]{:S(2)}) %collective-permute-start) | collective-permute-done | bytes 786464 | tf_op jit(solution)/shard_map/while/body/eval_jaxpr/ppermute | solution.py:15
  158.7 2.4 multiply_add_fusion.7
  164.3 11.4 %collective-permute-done = bf16[2,384,512]{2,1,0:T(8,128)(2,1)S(1)} collective-permute-done((bf16[2,384,512]{2,1,0:T(8,128)(2,1)}, bf16[2,384,512]{2,1,0:T(8,128)(2,1)S(1)}, u32[]{:S(2)}, u32[]{:S(2)}) %collective-permute-start) | collective-permute-done | bytes 786464 | tf_op jit(solution)/shard_map/while/body/eval_jaxpr/ppermute | solution.py:15
  187.9 2.4 multiply_add_fusion.7
  193.5 11.4 %collective-permute-done = bf16[2,384,512]{2,1,0:T(8,128)(2,1)S(1)} collective-permute-done((bf16[2,384,512]{2,1,0:T(8,128)(2,1)}, bf16[2,384,512]{2,1,0:T(8,128)(2,1)S(1)}, u32[]{:S(2)}, u32[]{:S(2)}) %collective-permute-start) | collective-permute-done | bytes 786464 | tf_op jit(solution)/shard_map/while/body/eval_jaxpr/ppermute | solution.py:15
  217.2 2.4 multiply_add_fusion.7
  222.8 11.4 %collective-permute-done = bf16[2,384,512]{2,1,0:T(8,128)(2,1)S(1)} collective-permute-done((bf16[2,384,512]{2,1,0:T(8,128)(2,1)}, bf16[2,384,512]{2,1,0:T(8,128)(2,1)S(1)}, u32[]{:S(2)}, u32[]{:S(2)}) %collective-permute-start) | collective-permute-done | bytes 786464 | tf_op jit(solution)/shard_map/while/body/eval_jaxpr/ppermute | solution.py:15
  246.4 2.4 multiply_add_fusion.7
  252.1 11.4 %collective-permute-done = bf16[2,384,512]{2,1,0:T(8,128)(2,1)S(1)} collective-permute-done((bf16[2,384,512]{2,1,0:T(8,128)(2,1)}, bf16[2,384,512]{2,1,0:T(8,128)(2,1)S(1)}, u32[]{:S(2)}, u32[]{:S(2)}) %collective-permute-start) | collective-permute-done | bytes 786464 | tf_op jit(solution)/shard_map/while/body/eval_jaxpr/ppermute | solution.py:15
  275.7 2.4 multiply_add_fusion.7
  281.3 11.4 %collective-permute-done = bf16[2,384,512]{2,1,0:T(8,128)(2,1)S(1)} collective-permute-done((bf16[2,384,512]{2,1,0:T(8,128)(2,1)}, bf16[2,384,512]{2,1,0:T(8,128)(2,1)S(1)}, u32[]{:S(2)}, u32[]{:S(2)}) %collective-permute-start) | collective-permute-done | bytes 786464 | tf_op jit(solution)/shard_map/while/body/eval_jaxpr/ppermute | solution.py:15
  310.6 11.4 %collective-permute-done = bf16[2,384,512]{2,1,0:T(8,128)(2,1)S(1)} collective-permute-done((bf16[2,384,512]{2,1,0:T(8,128)(2,1)}, bf16[2,384,512]{2,1,0:T(8,128)(2,1)S(1)}, u32[]{:S(2)}, u32[]{:S(2)}) %collective-permute-start) | collective-permute-done | bytes 786464 | tf_op jit(solution)/shard_map/while/body/eval_jaxpr/ppermute | solution.py:15
  334.2 2.4 multiply_add_fusion.7
  339.8 11.4 %collective-permute-done = bf16[2,384,512]{2,1,0:T(8,128)(2,1)S(1)} collective-permute-done((bf16[2,384,512]{2,1,0:T(8,128)(2,1)}, bf16[2,384,512]{2,1,0:T(8,128)(2,1)S(1)}, u32[]{:S(2)}, u32[]{:S(2)}) %collective-permute-start) | collective-permute-done | bytes 786464 | tf_op jit(solution)/shard_map/while/body/eval_jaxpr/ppermute | solution.py:15
  369.1 11.4 %collective-permute-done = bf16[2,384,512]{2,1,0:T(8,128)(2,1)S(1)} collective-permute-done((bf16[2,384,512]{2,1,0:T(8,128)(2,1)}, bf16[2,384,512]{2,1,0:T(8,128)(2,1)S(1)}, u32[]{:S(2)}, u32[]{:S(2)}) %collective-permute-start) | collective-permute-done | bytes 786464 | tf_op jit(solution)/shard_map/while/body/eval_jaxpr/ppermute | solution.py:15
  392.7 2.4 multiply_add_fusion.7
  398.4 11.4 %collective-permute-done = bf16[2,384,512]{2,1,0:T(8,128)(2,1)S(1)} collective-permute-done((bf16[2,384,512]{2,1,0:T(8,128)(2,1)}, bf16[2,384,512]{2,1,0:T(8,128)(2,1)S(1)}, u32[]{:S(2)}, u32[]{:S(2)}) %collective-permute-start) | collective-permute-done | bytes 786464 | tf_op jit(solution)/shard_map/while/body/eval_jaxpr/ppermute | solution.py:15
  427.6 11.4 %collective-permute-done = bf16[2,384,512]{2,1,0:T(8,128)(2,1)S(1)} collective-permute-done((bf16[2,384,512]{2,1,0:T(8,128)(2,1)}, bf16[2,384,512]{2,1,0:T(8,128)(2,1)S(1)}, u32[]{:S(2)}, u32[]{:S(2)}) %collective-permute-start) | collective-permute-done | bytes 786464 | tf_op jit(solution)/shard_map/while/body/eval_jaxpr/ppermute | solution.py:15
  451.3 2.4 multiply_add_fusion.7
  456.9 11.4 %collective-permute-done = bf16[2,384,512]{2,1,0:T(8,128)(2,1)S(1)} collective-permute-done((bf16[2,384,512]{2,1,0:T(8,128)(2,1)}, bf16[2,384,512]{2,1,0:T(8,128)(2,1)S(1)}, u32[]{:S(2)}, u32[]{:S(2)}) %collective-permute-start) | collective-permute-done | bytes 786464 | tf_op jit(solution)/shard_map/while/body/eval_jaxpr/ppermute | solution.py:15
  480.5 2.4 multiply_add_fusion.7
  487.0 4.2 convolution_convert_fusion
  493.1 3.4 pad_maximum_fusion
  496.5 98.8 %reduce-scatter.2.cloned.1.call-done = bf16[48,8192]{1,0:T(8,128)(2,1)} async-done(((bf16[384,8192]{1,0:T(8,128)(2,1)}), bf16[48,8192]{1,0:T(8,128)(2,1)}) %reduce-scatter.2.cloned.1.call-update) | async-done | bytes 786448 | tf_op jit(solution)/shard_map/reduce_scatter | solution.py:154
  (424 shorter events, 248.0 us)
Async XLA Ops:
  6.5 588.8 %reduce-scatter.2.cloned.1.call-start = ((), (), s32[]{:S(2)}) async-start(), calls=%async_computation.1 | async-start | bytes 7077888 | tf_op jit(solution)/shard_map/reduce_scatter | solution.py:154
  7.2 2.9 copy-start.4
  36.2 3.5 copy-start.8
  42.9 1.7 copy-start.5
  42.9 1.7 copy-start.10
  42.9 1.7 copy-start.12
  44.8 13.8 %collective-permute-start = (bf16[2,384,512]{2,1,0:T(8,128)(2,1)}, bf16[2,384,512]{2,1,0:T(8,128)(2,1)S(1)}, u32[]{:S(2)}, u32[]{:S(2)}) collective-permute-start(bf16[2,384,512]{2,1,0:T(8,128)(2,1)} %get-tuple-element.532), channel_id=1, source_target_pairs={{0,8},{8,16},{16,24},{24,32},{32,40},{40,48},{48,56},{56,64},{64,7... | collective-permute-start | bytes 2359304 | tf_op jit(solution)/shard_map/while/body/eval_jaxpr/ppermute | solution.py:15
  66.1 1.6 copy-start.1
  74.2 13.7 %collective-permute-start = (bf16[2,384,512]{2,1,0:T(8,128)(2,1)}, bf16[2,384,512]{2,1,0:T(8,128)(2,1)S(1)}, u32[]{:S(2)}, u32[]{:S(2)}) collective-permute-start(bf16[2,384,512]{2,1,0:T(8,128)(2,1)} %get-tuple-element.532), channel_id=1, source_target_pairs={{0,8},{8,16},{16,24},{24,32},{32,40},{40,48},{48,56},{56,64},{64,7... | collective-permute-start | bytes 2359304 | tf_op jit(solution)/shard_map/while/body/eval_jaxpr/ppermute | solution.py:15
  95.4 1.6 copy-start.1
  103.4 13.7 %collective-permute-start = (bf16[2,384,512]{2,1,0:T(8,128)(2,1)}, bf16[2,384,512]{2,1,0:T(8,128)(2,1)S(1)}, u32[]{:S(2)}, u32[]{:S(2)}) collective-permute-start(bf16[2,384,512]{2,1,0:T(8,128)(2,1)} %get-tuple-element.532), channel_id=1, source_target_pairs={{0,8},{8,16},{16,24},{24,32},{32,40},{40,48},{48,56},{56,64},{64,7... | collective-permute-start | bytes 2359304 | tf_op jit(solution)/shard_map/while/body/eval_jaxpr/ppermute | solution.py:15
  124.6 1.6 copy-start.1
  132.7 13.7 %collective-permute-start = (bf16[2,384,512]{2,1,0:T(8,128)(2,1)}, bf16[2,384,512]{2,1,0:T(8,128)(2,1)S(1)}, u32[]{:S(2)}, u32[]{:S(2)}) collective-permute-start(bf16[2,384,512]{2,1,0:T(8,128)(2,1)} %get-tuple-element.532), channel_id=1, source_target_pairs={{0,8},{8,16},{16,24},{24,32},{32,40},{40,48},{48,56},{56,64},{64,7... | collective-permute-start | bytes 2359304 | tf_op jit(solution)/shard_map/while/body/eval_jaxpr/ppermute | solution.py:15
  161.9 13.7 %collective-permute-start = (bf16[2,384,512]{2,1,0:T(8,128)(2,1)}, bf16[2,384,512]{2,1,0:T(8,128)(2,1)S(1)}, u32[]{:S(2)}, u32[]{:S(2)}) collective-permute-start(bf16[2,384,512]{2,1,0:T(8,128)(2,1)} %get-tuple-element.532), channel_id=1, source_target_pairs={{0,8},{8,16},{16,24},{24,32},{32,40},{40,48},{48,56},{56,64},{64,7... | collective-permute-start | bytes 2359304 | tf_op jit(solution)/shard_map/while/body/eval_jaxpr/ppermute | solution.py:15
  183.1 1.6 copy-start.1
  191.2 13.7 %collective-permute-start = (bf16[2,384,512]{2,1,0:T(8,128)(2,1)}, bf16[2,384,512]{2,1,0:T(8,128)(2,1)S(1)}, u32[]{:S(2)}, u32[]{:S(2)}) collective-permute-start(bf16[2,384,512]{2,1,0:T(8,128)(2,1)} %get-tuple-element.532), channel_id=1, source_target_pairs={{0,8},{8,16},{16,24},{24,32},{32,40},{40,48},{48,56},{56,64},{64,7... | collective-permute-start | bytes 2359304 | tf_op jit(solution)/shard_map/while/body/eval_jaxpr/ppermute | solution.py:15
  220.5 13.7 %collective-permute-start = (bf16[2,384,512]{2,1,0:T(8,128)(2,1)}, bf16[2,384,512]{2,1,0:T(8,128)(2,1)S(1)}, u32[]{:S(2)}, u32[]{:S(2)}) collective-permute-start(bf16[2,384,512]{2,1,0:T(8,128)(2,1)} %get-tuple-element.532), channel_id=1, source_target_pairs={{0,8},{8,16},{16,24},{24,32},{32,40},{40,48},{48,56},{56,64},{64,7... | collective-permute-start | bytes 2359304 | tf_op jit(solution)/shard_map/while/body/eval_jaxpr/ppermute | solution.py:15
  241.7 1.6 copy-start.1
  249.7 13.7 %collective-permute-start = (bf16[2,384,512]{2,1,0:T(8,128)(2,1)}, bf16[2,384,512]{2,1,0:T(8,128)(2,1)S(1)}, u32[]{:S(2)}, u32[]{:S(2)}) collective-permute-start(bf16[2,384,512]{2,1,0:T(8,128)(2,1)} %get-tuple-element.532), channel_id=1, source_target_pairs={{0,8},{8,16},{16,24},{24,32},{32,40},{40,48},{48,56},{56,64},{64,7... | collective-permute-start | bytes 2359304 | tf_op jit(solution)/shard_map/while/body/eval_jaxpr/ppermute | solution.py:15
  270.9 1.6 copy-start.1
  279.0 13.7 %collective-permute-start = (bf16[2,384,512]{2,1,0:T(8,128)(2,1)}, bf16[2,384,512]{2,1,0:T(8,128)(2,1)S(1)}, u32[]{:S(2)}, u32[]{:S(2)}) collective-permute-start(bf16[2,384,512]{2,1,0:T(8,128)(2,1)} %get-tuple-element.532), channel_id=1, source_target_pairs={{0,8},{8,16},{16,24},{24,32},{32,40},{40,48},{48,56},{56,64},{64,7... | collective-permute-start | bytes 2359304 | tf_op jit(solution)/shard_map/while/body/eval_jaxpr/ppermute | solution.py:15
  300.2 1.6 copy-start.1
  308.2 13.7 %collective-permute-start = (bf16[2,384,512]{2,1,0:T(8,128)(2,1)}, bf16[2,384,512]{2,1,0:T(8,128)(2,1)S(1)}, u32[]{:S(2)}, u32[]{:S(2)}) collective-permute-start(bf16[2,384,512]{2,1,0:T(8,128)(2,1)} %get-tuple-element.532), channel_id=1, source_target_pairs={{0,8},{8,16},{16,24},{24,32},{32,40},{40,48},{48,56},{56,64},{64,7... | collective-permute-start | bytes 2359304 | tf_op jit(solution)/shard_map/while/body/eval_jaxpr/ppermute | solution.py:15
  337.5 13.7 %collective-permute-start = (bf16[2,384,512]{2,1,0:T(8,128)(2,1)}, bf16[2,384,512]{2,1,0:T(8,128)(2,1)S(1)}, u32[]{:S(2)}, u32[]{:S(2)}) collective-permute-start(bf16[2,384,512]{2,1,0:T(8,128)(2,1)} %get-tuple-element.532), channel_id=1, source_target_pairs={{0,8},{8,16},{16,24},{24,32},{32,40},{40,48},{48,56},{56,64},{64,7... | collective-permute-start | bytes 2359304 | tf_op jit(solution)/shard_map/while/body/eval_jaxpr/ppermute | solution.py:15
  358.7 1.6 copy-start.1
  366.8 13.7 %collective-permute-start = (bf16[2,384,512]{2,1,0:T(8,128)(2,1)}, bf16[2,384,512]{2,1,0:T(8,128)(2,1)S(1)}, u32[]{:S(2)}, u32[]{:S(2)}) collective-permute-start(bf16[2,384,512]{2,1,0:T(8,128)(2,1)} %get-tuple-element.532), channel_id=1, source_target_pairs={{0,8},{8,16},{16,24},{24,32},{32,40},{40,48},{48,56},{56,64},{64,7... | collective-permute-start | bytes 2359304 | tf_op jit(solution)/shard_map/while/body/eval_jaxpr/ppermute | solution.py:15
  396.0 13.7 %collective-permute-start = (bf16[2,384,512]{2,1,0:T(8,128)(2,1)}, bf16[2,384,512]{2,1,0:T(8,128)(2,1)S(1)}, u32[]{:S(2)}, u32[]{:S(2)}) collective-permute-start(bf16[2,384,512]{2,1,0:T(8,128)(2,1)} %get-tuple-element.532), channel_id=1, source_target_pairs={{0,8},{8,16},{16,24},{24,32},{32,40},{40,48},{48,56},{56,64},{64,7... | collective-permute-start | bytes 2359304 | tf_op jit(solution)/shard_map/while/body/eval_jaxpr/ppermute | solution.py:15
  417.2 1.6 copy-start.1
  425.3 13.7 %collective-permute-start = (bf16[2,384,512]{2,1,0:T(8,128)(2,1)}, bf16[2,384,512]{2,1,0:T(8,128)(2,1)S(1)}, u32[]{:S(2)}, u32[]{:S(2)}) collective-permute-start(bf16[2,384,512]{2,1,0:T(8,128)(2,1)} %get-tuple-element.532), channel_id=1, source_target_pairs={{0,8},{8,16},{16,24},{24,32},{32,40},{40,48},{48,56},{56,64},{64,7... | collective-permute-start | bytes 2359304 | tf_op jit(solution)/shard_map/while/body/eval_jaxpr/ppermute | solution.py:15
  454.5 13.7 %collective-permute-start = (bf16[2,384,512]{2,1,0:T(8,128)(2,1)}, bf16[2,384,512]{2,1,0:T(8,128)(2,1)S(1)}, u32[]{:S(2)}, u32[]{:S(2)}) collective-permute-start(bf16[2,384,512]{2,1,0:T(8,128)(2,1)} %get-tuple-element.532), channel_id=1, source_target_pairs={{0,8},{8,16},{16,24},{24,32},{32,40},{40,48},{48,56},{56,64},{64,7... | collective-permute-start | bytes 2359304 | tf_op jit(solution)/shard_map/while/body/eval_jaxpr/ppermute | solution.py:15
  475.7 1.6 copy-start.1
  487.0 4.2 copy-start.2
  (39 other events, 44.6 us)
Sparse Core Ops, SparseCore 0:
  496.6 98.6 reduce-scatter.1
where the time goes:
time: 605 us; the launch traced here: 602 us
  waiting for transfers between devices  270 us (45%)
  local copies, waits for them, and re-layouts  141 us (23%)
  matrix products  108 us (18%)
  other arithmetic  48.3 us (8%)
  loops' own time  20.4 us (3%)
  between operations  14.9 us (2%)
    ppermute x15, waiting for transfers between devices, shifted(): return lax.ppermute(value, axis, pairs)  171 us
    reduce_scatter x1, waiting for transfers between devices, shards(): lax.psum_scatter(summands.astype(jnp.bfloat16), 'head', scatter_dimension...  98.8 us
    dot_general x32, matrix products, attend(): jnp.einsum('hqk,khd->hqd', weights.astype(jnp.bfloat16), value_rows, pref...  53.6 us
    squeeze x30, local copies, waits for them, and re-layouts, attend(): value_rows = key_values[1].reshape(-1, local_heads, HEAD_SIZE)  49.5 us
    squeeze x30, local copies, waits for them, and re-layouts, attend(): key_rows = key_values[0].reshape(-1, local_heads, HEAD_SIZE)  49.4 us
    dot_general x32, matrix products, attend(): jnp.einsum('qhd,khd->hqk', queries, key_rows, preferred_element_type=jnp....  34.6 us
    another operation x1, loops' own time, shards(): lax.fori_loop(1, ctx_count, cycle_turn, (clean_pair, carried))  20.4 us
    reduce_sum x16, other arithmetic, attend(): new_sum = old_sum * factor + weights.sum(axis=-1)  19.4 us
  transfers between devices with their start and end apart: 16, of which 16 were waited for; matrix products, arithmetic and copies ran while one was open for 3% of the time, Pallas kernels for 0%

commit v1 on v0

v1 whole, which is shorter than its diff:
```python
import functools
import math

import jax
import jax.numpy as jnp
from jax import lax
from jax.experimental import pallas as pl
from jax.experimental.pallas import tpu as pltpu
from jax.sharding import PartitionSpec as P

MESH = pl.DeviceIdType.MESH
HEAD = 128
ROWS = 384
HALF = 192
BLOCK = 64
QT = 208
NEG = -1e30
LOG2_SCALE = math.log2(math.e) / math.sqrt(HEAD)
F32 = jnp.float32
BF16 = jnp.bfloat16


def coords():
    i = lax.axis_index("ctx")
    j = lax.axis_index("head")
    return j // 2, i // 4, (i // 2) % 2, j % 2, i % 2


def ctx_of(y, zl, c):
    return (y * 2 + zl) * 2 + c


def rcopy(src, dst, ssem, rsem, dev):
    return pltpu.make_async_remote_copy(
        src_ref=src, dst_ref=dst, send_sem=ssem, recv_sem=rsem, device_id=dev, device_id_type=MESH
    )


def greet(devs):
    barrier = pltpu.get_barrier_semaphore()
    for dev in devs:
        pl.semaphore_signal(barrier, inc=1, device_id=dev, device_id_type=MESH)
    return lambda: pl.semaphore_wait(barrier, len(devs))


def project_kernel(
    act, nmask, mvec, w, wo,
    kv, q, mproj, msk, wq,
    lhs, wbuf, kvst, qst, lsem, wsem,
    y_s, y_r, q_s, q_r, m_s, m_r, z_s, c_s, f_r, x_s, x_r,
):
    x, y, zl, zh, c = coords()
    hd = lax.axis_index("head")
    me = ctx_of(y, zl, c)
    ydev = [(ctx_of(lax.rem(y + k, 4), zl, c), hd) for k in range(4)]
    zdev = (ctx_of(y, 1 - zl, c), hd)
    cdev = (ctx_of(y, zl, 1 - c), hd)
    xdev = (me, lax.rem(x + 2, 4) * 2 + zh)
    arrive = greet([ydev[1], ydev[2], ydev[3], zdev, cdev, xdev])

    act_in = pltpu.make_async_copy(act, lhs.at[pl.ds(0, ROWS)], lsem)
    act_in.start()
    order = (0, 1, 3, 2)
    win = []
    for n, k in enumerate(order):
        col = pl.multiple_of(lax.rem(y + k, 4) * HEAD, HEAD)
        group = []
        for part, m in enumerate((1, 2, 0)):
            cp = pltpu.make_async_copy(
                w.at[m, :, pl.ds(col, HEAD)],
                wbuf.at[n, :, pl.ds(part * HEAD, HEAD)],
                wsem.at[n, part],
            )
            cp.start()
            group.append(cp)
        win.append(group)
    lhs[pl.ds(ROWS, 16), :] = jnp.broadcast_to(mvec[...], (16, 4096))
    msk[y] = jnp.broadcast_to(nmask[...].astype(F32), (8, ROWS))
    act_in.wait()

    sends = []

    def start(cp):
        cp.start()
        sends.append(cp)

    qd = lax.rem(y, 2) * 2 + c
    qsends = []
    for n, k in enumerate(order):
        for cp in win[n]:
            cp.wait()
        if n == 0:
            r = jnp.dot(lhs[...], wbuf[0], preferred_element_type=F32)
            kv[me] = r[:ROWS, : 2 * HEAD].astype(BF16)
            q[y] = (r[:ROWS, 2 * HEAD :] * LOG2_SCALE).astype(BF16)
            mproj[:, : 2 * HEAD] = r[ROWS:, : 2 * HEAD].astype(BF16)
            mproj[:, 2 * HEAD :] = (r[ROWS:, 2 * HEAD :] * LOG2_SCALE).astype(BF16)
            arrive()
            start(rcopy(kv.at[me], kv.at[me], z_s.at[0], f_r.at[me], zdev))
            start(rcopy(kv.at[me], kv.at[me], c_s.at[0], f_r.at[me], cdev))
            qcol = pl.multiple_of(qd * 1024, 1024)
            start(rcopy(wo.at[:, pl.ds(qcol, 1024)], wq, x_s, x_r, xdev))
            for k2 in (1, 3, 2):
                start(rcopy(msk.at[y], msk.at[y], m_s.at[k2 - 1], m_r.at[y], ydev[k2]))
        else:
            r = jnp.dot(lhs[pl.ds(0, ROWS), :], wbuf[n], preferred_element_type=F32)
            kvst[n - 1] = r[:, : 2 * HEAD].astype(BF16)
            qst[n - 1] = (r[:, 2 * HEAD :] * LOG2_SCALE).astype(BF16)
            start(rcopy(kvst.at[n - 1], kv.at[me], y_s.at[n - 1], f_r.at[me], ydev[k]))
            qsends.append(rcopy(qst.at[n - 1], q.at[y], q_s.at[n - 1], q_r.at[y], ydev[k]))
    for cp in qsends:
        start(cp)

    def landed(slot):
        rcopy(kv.at[slot], kv.at[slot], z_s.at[0], f_r.at[slot], cdev).wait_recv()

    def from_y(n, k):
        slot = ctx_of(lax.rem(y + k, 4), zl, c)
        landed(slot)
        start(rcopy(kv.at[slot], kv.at[slot], z_s.at[n], f_r.at[slot], zdev))
        start(rcopy(kv.at[slot], kv.at[slot], c_s.at[n], f_r.at[slot], cdev))

    def from_z(n, k):
        slot = ctx_of(lax.rem(y + k, 4), 1 - zl, c)
        landed(slot)
        start(rcopy(kv.at[slot], kv.at[slot], c_s.at[4 + n], f_r.at[slot], cdev))

    from_y(1, 1)
    from_z(0, 0)
    from_y(2, 3)
    from_z(1, 1)
    from_y(3, 2)
    from_z(2, 3)
    from_z(3, 2)
    for k in order:
        for z2 in range(2):
            landed(ctx_of(lax.rem(y + k, 4), z2, 1 - c))
    for k in (1, 3, 2):
        yk = lax.rem(y + k, 4)
        rcopy(q.at[yk], q.at[yk], q_s.at[0], q_r.at[yk], cdev).wait_recv()
        rcopy(msk.at[yk], msk.at[yk], m_s.at[0], m_r.at[yk], cdev).wait_recv()
    rcopy(wo.at[:, pl.ds(0, 1024)], wq, x_s, x_r, xdev).wait_recv()
    for cp in sends:
        cp.wait_send()


def attend_kernel(span, kv, q, mproj, msk, keyspan, out, qt, vx, m_ref, o_ref):
    x, y, zl, zh, c = coords()
    p_x = x // 2
    ones = jnp.ones((ROWS, HEAD), BF16)
    for s in range(16):
        vx[pl.ds(s * ROWS, ROWS), pl.ds(0, HEAD)] = kv[s, :, HEAD:]
        vx[pl.ds(s * ROWS, ROWS), pl.ds(HEAD, HEAD)] = ones
    for s in range(4):
        for h in range(2):
            qt[2 * s + h, pl.ds(0, HALF), :] = q[s, pl.ds(h * HALF, HALF), :]
            qt[2 * s + h, pl.ds(HALF, 16), :] = mproj[:, 2 * HEAD :]
    km = mproj[:, :HEAD]
    vm = mproj[pl.ds(0, 1), pl.ds(HEAD, HEAD)].astype(F32)
    vm = jnp.concatenate([vm, jnp.ones((1, HEAD), F32)], axis=1)

    rowi = lax.broadcasted_iota(jnp.int32, (QT, HALF), 0)
    coli = lax.broadcasted_iota(jnp.int32, (QT, HALF), 1)
    bi = jnp.where(rowi < HALF, rowi // BLOCK, jnp.minimum(rowi - HALF, 2))
    bj = coli // BLOCK

    def one(i, _):
        s = i // 2
        h = lax.rem(i, 2)
        src = ctx_of(s, zl, c)
        u = span[2 * src + h]
        qi = qt[i]
        m_ref[...] = jnp.full((QT, HEAD), NEG, F32)
        o_ref[...] = jnp.zeros((QT, 2 * HEAD), F32)

        def keys(g, _):
            k = kv[pl.ds(4 * g, 4), :, :HEAD].reshape(4 * ROWS, HEAD)
            sc = lax.dot_general(qi, k, (((1,), (1,)), ((), ())), preferred_element_type=F32)
            ks = keyspan[g]
            sc = sc + jnp.where(ks < u, F32(0), F32(NEG))
            old = m_ref[:, :1]
            new = jnp.maximum(old, jnp.max(sc, axis=1, keepdims=True))
            p = jnp.exp2(sc - new).astype(BF16)
            start_row = pl.multiple_of(g * 4 * ROWS, 4 * ROWS)
            pv = jnp.dot(p, vx[pl.ds(start_row, 4 * ROWS), :], preferred_element_type=F32)
            o_ref[...] = o_ref[...] * jnp.exp2(old - new) + pv
            m_ref[...] = jnp.broadcast_to(new, (QT, HEAD))
            return 0

        lax.fori_loop(0, 4, keys, 0)

        row0 = pl.multiple_of(h * HALF, HALF)
        ko = kv[src, pl.ds(row0, HALF), :HEAD]
        vstart = pl.multiple_of(src * ROWS + h * HALF, HALF)
        vo = vx[pl.ds(vstart, HALF), :]
        so = lax.dot_general(qi, ko, (((1,), (1,)), ((), ())), preferred_element_type=F32)
        sm = lax.dot_general(qi, km, (((1,), (1,)), ((), ())), preferred_element_type=F32)[:, :1]
        mrow = jnp.where(h == 0, msk[s, pl.ds(0, 1), pl.ds(0, HALF)], msk[s, pl.ds(0, 1), pl.ds(HALF, HALF)])
        mp = m_ref[:, :1]
        op = o_ref[...]

        sc = jnp.where(bj <= bi, so, F32(NEG))
        mc = jnp.maximum(mp, jnp.max(sc, axis=1, keepdims=True))
        pc = jnp.where(bj <= bi, jnp.exp2(sc - mc), F32(0)).astype(BF16)
        oc = op * jnp.exp2(mp - mc) + jnp.dot(pc, vo, preferred_element_type=F32)
        clean = (oc[:HALF, :HEAD] / oc[:HALF, HEAD:]).astype(BF16)

        hit = (bj == bi) & (mrow > 0.5)
        sn = jnp.where(hit, sm, sc)
        mn = jnp.maximum(mp, jnp.max(sn, axis=1, keepdims=True))
        pn = jnp.where(bj <= bi, jnp.exp2(sn - mn), F32(0)).astype(BF16)
        pz = jnp.where(hit, F32(0), pn.astype(F32))
        wm = jnp.sum(pn.astype(F32) - pz, axis=1, keepdims=True)
        on = op * jnp.exp2(mp - mn) + jnp.dot(pz.astype(BF16), vo, preferred_element_type=F32) + wm * vm
        an = on[:, :HEAD] / on[:, HEAD:]
        mcol = jnp.sum(jnp.where(rowi == coli, mrow, F32(0)), axis=1, keepdims=True)[:HALF]
        masked = jnp.concatenate(
            [jnp.broadcast_to(an[HALF + b : HALF + b + 1], (BLOCK, HEAD)) for b in range(3)], axis=0
        )
        noisy = jnp.where(mcol > 0.5, masked, an[:HALF]).astype(BF16)

        for b in range(4):
            xo = 2 * h + b // 2
            zo = b % 2
            near = (zo == p_x)
            side = jnp.where(near, lax.rem(x + 1, 4), lax.rem(x + 3, 4))
            pos = jnp.where(
                xo == x,
                zo,
                jnp.where(
                    xo == lax.rem(x + 2, 4),
                    4 + zo,
                    jnp.where(near, 0, 4) + jnp.where(xo == side, 2, 3),
                ),
            )
            out[s, pos, pl.ds(0, 48), :] = clean[b * 48 : (b + 1) * 48]
            out[s, pos, pl.ds(48, 48), :] = noisy[b * 48 : (b + 1) * 48]
        return 0

    lax.fori_loop(0, 8, one, 0)


def mix_kernel(
    att, wo, wq, out,
    abuf, wown, wp, keep, xs, xr, zs, zr,
    l_sem, o_sem, a_s, a_r, wq_l, wc_s, wc_r, wy_s, wy_r, wf_s, wf_r, x_s, x_r, z_s, z_r,
):
    x, y, zl, zh, c = coords()
    hd = lax.axis_index("head")
    me = ctx_of(y, zl, c)
    x2 = lax.rem(x + 2, 4)
    adev = {}
    for t, xt in ((0, x), (1, x2)):
        for k in range(4):
            adev[t, k] = (ctx_of(lax.rem(y + k, 4), zl, c), xt * 2 + zh)
    cdev = (ctx_of(y, zl, 1 - c), hd)
    xup = (me, lax.rem(x + 1, 4) * 2 + zh)
    xdn = (me, lax.rem(x + 3, 4) * 2 + zh)
    zdev = (me, x * 2 + 1 - zh)
    wyk = lax.rem(y + 1 + 2 * c, 4)
    wydev = (ctx_of(wyk, zl, c), hd)
    arrive = greet([adev[t, k] for t in range(2) for k in range(4) if (t, k) != (0, 0)] + [cdev, xup, xdn, zdev])

    qd = lax.rem(y, 2) * 2 + c
    order = (qd, qd + 1 - 2 * c, lax.rem(qd + 2, 4), lax.rem(qd + 2, 4) + 1 - 2 * c)
    lcopy = []
    own_col = pl.multiple_of(y * HEAD, HEAD)
    cp = pltpu.make_async_copy(att.at[y, pl.ds(0, 4)], abuf.at[:, :, pl.ds(own_col, HEAD)], l_sem)
    cp.start()
    lcopy.append(cp)
    wl = []
    for n in range(4):
        col = pl.multiple_of(order[n] * 1024, 1024)
        cp = pltpu.make_async_copy(wo.at[:, pl.ds(col, 1024)], wown.at[n], o_sem.at[n])
        cp.start()
        wl.append(cp)
    wpl = pltpu.make_async_copy(wq, wp.at[0], wq_l)
    wpl.start()
    arrive()
    sends = []

    def start(cp):
        cp.start()
        sends.append(cp)

    for n, (t, k) in enumerate([(0, 2), (1, 2), (0, 1), (0, 3), (1, 1), (1, 3), (1, 0)]):
        yk = lax.rem(y + k, 4)
        dcol = pl.multiple_of((4 * t + y) * HEAD, HEAD)
        start(
            rcopy(
                att.at[yk, pl.ds(4 * t, 4)],
                abuf.at[:, :, pl.ds(dcol, HEAD)],
                a_s.at[n],
                a_r.at[4 * t + y],
                adev[t, k],
            )
        )
    wpl.wait()
    start(rcopy(wp.at[0], wp.at[1], wc_s, wc_r, cdev))
    for t, k in [(0, 1), (0, 3), (1, 0), (0, 2), (1, 1), (1, 3), (1, 2)]:
        yk = lax.rem(y + k, 4)
        dcol = pl.multiple_of((4 * t + yk) * HEAD, HEAD)
        rcopy(
            att.at[0, pl.ds(0, 4)], abuf.at[:, :, pl.ds(dcol, HEAD)], a_s.at[0], a_r.at[4 * t + yk], cdev
        ).wait_recv()
    for e in range(2):
        src = wp.at[0, :, pl.ds(e * 512, 512)]
        start(rcopy(src, wp.at[2, :, pl.ds(e * 512, 512)], wy_s.at[e], wy_r.at[e], wydev))
    for cp in lcopy:
        cp.wait()

    def matmul(n):
        j, e = n // 2, n % 2
        if e == 0:
            wl[j].wait()
        cols = pl.ds(e * 512, 512)
        if j == 1 and e == 0:
            rcopy(wp.at[0], wp.at[1], wc_s, wc_r, cdev).wait_recv()
        if j == 2:
            half = wp.at[2, :, cols]
            rcopy(half, half, wy_s.at[e], wy_r.at[e], cdev).wait_recv()
            start(rcopy(half, wp.at[3, :, cols], wf_s.at[e], wf_r.at[e], cdev))
        if j == 3:
            half = wp.at[3, :, cols]
            rcopy(half, half, wf_s.at[e], wf_r.at[e], cdev).wait_recv()
        a = abuf[...].reshape(ROWS, 1024)
        r = jnp.dot(a[:, :512], wown[j, :, cols], preferred_element_type=F32)
        r = r + jnp.dot(a[:, 512:], wp[j, :, cols], preferred_element_type=F32)
        keep[n] = r[:192].reshape(2, 96, 512)
        xs[n, 0] = r[192:288].astype(BF16)
        xs[n, 1] = r[288:].astype(BF16)
        start(rcopy(xs.at[n, 0], xr.at[n, 0], x_s.at[n, 0], x_r.at[n, 0], xup))
        start(rcopy(xs.at[n, 1], xr.at[n, 1], x_s.at[n, 1], x_r.at[n, 1], xdn))

    from_below = lax.rem(x + 3, 4) // 2

    def reduce_x(n):
        for d in range(2):
            rcopy(xs.at[n, d], xr.at[n, d], x_s.at[n, d], x_r.at[n, d], xup).wait_recv()
        far = 1 - zh
        keep[n, zh] = keep[n, zh] + xr[n, (zh + from_below) % 2].astype(F32)
        zs[n] = (keep[n, far] + xr[n, (far + from_below) % 2].astype(F32)).astype(BF16)
        start(rcopy(zs.at[n], zr.at[n], z_s.at[n], z_r.at[n], zdev))

    def reduce_z(n):
        rcopy(zs.at[n], zr.at[n], z_s.at[n], z_r.at[n], zdev).wait_recv()
        total = (keep[n, zh] + zr[n].astype(F32)).astype(BF16)
        col = pl.multiple_of(order[n // 2] * 1024 + (n % 2) * 512, 512)
        out[:, pl.ds(col, 512)] = total[:48]
        out[:, pl.ds(4096 + col, 512)] = total[48:]

    for n in range(4):
        matmul(n)
    reduce_x(0)
    reduce_x(1)
    matmul(4)
    reduce_x(2)
    matmul(5)
    reduce_z(0)
    reduce_x(3)
    matmul(6)
    reduce_z(1)
    reduce_x(4)
    matmul(7)
    reduce_z(2)
    reduce_x(5)
    reduce_z(3)
    reduce_x(6)
    reduce_z(4)
    reduce_x(7)
    for n in (5, 6, 7):
        reduce_z(n)
    for cp in sends:
        cp.wait_send()


def vmem():
    return pl.BlockSpec(memory_space=pltpu.VMEM)


def anyspace():
    return pl.BlockSpec(memory_space=pl.ANY)


def shards(activations, noise_mask, span_order, mask_vector, input_weights, output_weight):
    dma = pltpu.SemaphoreType.DMA
    params = functools.partial(pltpu.CompilerParams, has_side_effects=True, vmem_limit_bytes=56 << 20)
    kv, q, mproj, msk, wq = pl.pallas_call(
        project_kernel,
        out_shape=(
            jax.ShapeDtypeStruct((16, ROWS, 2 * HEAD), BF16),
            jax.ShapeDtypeStruct((4, ROWS, HEAD), BF16),
            jax.ShapeDtypeStruct((16, 3 * HEAD), BF16),
            jax.ShapeDtypeStruct((4, 8, ROWS), F32),
            jax.ShapeDtypeStruct((512, 1024), BF16),
        ),
        in_specs=[anyspace(), vmem(), vmem(), anyspace(), anyspace()],
        out_specs=(vmem(), vmem(), vmem(), vmem(), anyspace()),
        scratch_shapes=[
            pltpu.VMEM((ROWS + 16, 4096), BF16),
            pltpu.VMEM((4, 4096, 3 * HEAD), BF16),
            pltpu.VMEM((3, ROWS, 2 * HEAD), BF16),
            pltpu.VMEM((3, ROWS, HEAD), BF16),
            dma,
            dma((4, 3)),
            dma((3,)),
            dma((16,)),
            dma((3,)),
            dma((4,)),
            dma((3,)),
            dma((4,)),
            dma((4,)),
            dma((8,)),
            dma((16,)),
            dma,
            dma,
        ],
        compiler_params=params(collective_id=1),
        name="project",
    )(
        activations,
        noise_mask.reshape(1, ROWS),
        mask_vector.reshape(1, 4096),
        input_weights,
        output_weight,
    )
    keyspan = jnp.repeat(span_order, HALF).reshape(4, 1, 4 * ROWS)
    att = pl.pallas_call(
        attend_kernel,
        out_shape=jax.ShapeDtypeStruct((4, 8, 96, HEAD), BF16),
        in_specs=[pl.BlockSpec(memory_space=pltpu.SMEM)] + [vmem()] * 5,
        out_specs=vmem(),
        scratch_shapes=[
            pltpu.VMEM((8, QT, HEAD), BF16),
            pltpu.VMEM((16 * ROWS, 2 * HEAD), BF16),
            pltpu.VMEM((QT, HEAD), F32),
            pltpu.VMEM((QT, 2 * HEAD), F32),
        ],
        compiler_params=pltpu.CompilerParams(vmem_limit_bytes=48 << 20),
        name="attend",
    )(span_order, kv, q, mproj, msk, keyspan)
    return pl.pallas_call(
        mix_kernel,
        out_shape=jax.ShapeDtypeStruct((48, 8192), BF16),
        in_specs=[vmem(), anyspace(), anyspace()],
        out_specs=vmem(),
        scratch_shapes=[
            pltpu.VMEM((4, 96, 1024), BF16),
            pltpu.VMEM((4, 512, 1024), BF16),
            pltpu.VMEM((4, 512, 1024), BF16),
            pltpu.VMEM((8, 2, 96, 512), F32),
            pltpu.VMEM((8, 2, 96, 512), BF16),
            pltpu.VMEM((8, 2, 96, 512), BF16),
            pltpu.VMEM((8, 96, 512), BF16),
            pltpu.VMEM((8, 96, 512), BF16),
            dma,
            dma((4,)),
            dma((7,)),
            dma((8,)),
            dma,
            dma,
            dma,
            dma((2,)),
            dma((2,)),
            dma((2,)),
            dma((2,)),
            dma((8, 2)),
            dma((8, 2)),
            dma((8,)),
            dma((8,)),
        ],
        compiler_params=params(collective_id=2),
        name="mix",
    )(att, output_weight, wq)


def solution(mesh):
    in_specs = (P("ctx", None), P("ctx"), P(), P(), P(None, None, "head"), P("head", None))
    out_specs = P(("ctx", "head"), None)
    return jax.shard_map(shards, mesh=mesh, in_specs=in_specs, out_specs=out_specs, check_vma=False)
```

time: 605 us -> 138 us (0.23)
  waiting for transfers between devices: 270 us -> 0 us
  local copies, waits for them, and re-layouts: 141 us -> 10.8 us
  Pallas kernels: 0 us -> 127 us
  matrix products: 108 us -> 0 us
  other arithmetic: 48.3 us -> 0 us
  loops' own time: 20.4 us -> 0 us
  between operations: 14.9 us -> 0.07 us
    ppermute x15 -> x0, waiting for transfers between devices: 171 us -> none  [shifted(): return lax.ppermute(value, axis, pairs)]
    pallas_call x0 -> x3, Pallas kernels: none -> 127 us  [the longest x1 48.4 us: shards(): pl.pallas_call(mix_kernel, out_shape=jax.ShapeDtypeStruct((48, 8192), BF1...]
    dot_general x69 -> x0, matrix products: 108 us -> none  [the longest x32 53.6 us: attend(): jnp.einsum('hqk,khd->hqd', weights.astype(jnp.bfloat16), value_rows, pref...]
    squeeze x60 -> x0, local copies, waits for them, and re-layouts: 98.9 us -> none  [the longest x30 49.5 us: attend(): value_rows = key_values[1].reshape(-1, local_heads, HEAD_SIZE)]
    reduce_scatter x1 -> x0, waiting for transfers between devices: 98.8 us -> none  [shards(): lax.psum_scatter(summands.astype(jnp.bfloat16), 'head', scatter_dimension...]
    reduce_sum x34 -> x0, other arithmetic: 31.7 us -> none  [the longest x16 19.4 us: attend(): new_sum = old_sum * factor + weights.sum(axis=-1)]
    another operation x1 -> x0, loops' own time: 20.4 us -> none  [shards(): lax.fori_loop(1, ctx_count, cycle_turn, (clean_pair, carried))]
    while x121 -> x0, local copies, waits for them, and re-layouts: 19.2 us -> none
  transfers between devices with their start and end apart: 16 -> 0, of which waited for: 16 -> 0; matrix products, arithmetic and copies ran while one was open for 3% -> 0% of each run, Pallas kernels for 0% -> 0%
where the time goes in v1:
time: 138 us
  Pallas kernels  127 us (92%)
  local copies, waits for them, and re-layouts  10.8 us (8%)
    pallas_call x1, Pallas kernels, shards(): pl.pallas_call(mix_kernel, out_shape=jax.ShapeDtypeStruct((48, 8192), BF1...  48.4 us
    pallas_call x1, Pallas kernels, shards(): pl.pallas_call(attend_kernel, out_shape=jax.ShapeDtypeStruct((4, 8, 96, H...  41.2 us
    pallas_call x1, Pallas kernels, shards(): pl.pallas_call(project_kernel, out_shape=(jax.ShapeDtypeStruct((16, ROWS,...  37.5 us
    unnamed x13, local copies, waits for them, and re-layouts  7.33 us

profile of v1, /device:TPU:0, one launch (start us, length us, event | category | flops | bytes accessed | tf_op | source)
XLA Modules:
  0.0 138.0 jit_solution(7565851132737119853)
XLA Ops:
  0.0 1.3 reshape.13.nmask
  1.3 0.7 broadcast_in_dim.7
  2.0 1.3 reshape.14.mvec
  3.3 0.1 broadcast_in_dim.8
  3.4 0.1 broadcast_in_dim.9.keyspan
  3.5 0.0 copy-start.5
  3.5 37.5 %project.1 = (bf16[16,384,256]{2,1,0:T(8,128)(2,1)}, bf16[4,384,128]{2,1,0:T(8,128)(2,1)}, bf16[16,384]{1,0:T(8,128)(2,1)}, f32[4,8,384]{2,1,0:T(8,128)}, bf16[512,1024]{1,0:T(8,128)(2,1)}) custom-call(bf16[384,4096]{1,0:T(8,128)(2,1)} %act.1, s32[1,384]{1,0:T(1,128)} %reshape.13.nmask, bf16[1,4096]{1,0:T(2,128)(2,1)} %reshape.14.mvec, ...), custom_call_target="tpu_custom_call" | custom-call | tf_op jit(solution)/shard_map/project/pallas_call | solution.py:388
  41.0 0.0 copy-done.5
  41.1 0.0 copy-start
  41.1 1.9 %copy-done = bf16[16,384,256]{2,1,0:T(8,128)(2,1)S(1)} copy-done((bf16[16,384,256]{2,1,0:T(8,128)(2,1)S(1)}, bf16[16,384,256]{2,1,0:T(8,128)(2,1)}, u32[]{:S(2)}) %copy-start) | copy-done | bytes 3145752
  42.9 0.0 copy-start.2
  42.9 1.0 copy-done.2
  43.9 0.0 copy-start.3
  43.9 0.8 copy-done.3
  44.7 0.0 copy-start.4
  44.7 0.7 copy-done.4
  45.4 41.2 %attend.1.att = bf16[4,8,96,128]{3,2,1,0:T(8,128)(2,1)S(1)} custom-call(s32[32]{0:T(128)S(1)} %copy-done.5, bf16[16,384,256]{2,1,0:T(8,128)(2,1)S(1)} %copy-done, bf16[4,384,128]{2,1,0:T(8,128)(2,1)S(1)} %copy-done.2, bf16[16,384]{1,0:T(8,128)(2,1)S(1)} %copy-done.4, f32[4,8,384]{2,1,0:T(8,128)S(1)} %copy-done.3, s32[4,1,1536]{2,1,0:T(1,128)S(1)} %broadcast_in_dim.9.keyspan), custom_call_target="tpu_custom_call" | custom-call | tf_op jit(solution)/shard_map/attend/pallas_call | solution.py:428
  86.7 0.0 copy-start.1
  86.7 0.9 copy-done.1
  87.5 48.4 %mix.1 = bf16[48,8192]{1,0:T(8,128)(2,1)} custom-call(bf16[4,8,96,128]{3,2,1,0:T(8,128)(2,1)} %copy-done.1, bf16[512,4096]{1,0:T(8,128)(2,1)} %wo.3, bf16[512,1024]{1,0:T(8,128)(2,1)} %get-tuple-element.14.wq), custom_call_target="tpu_custom_call" | custom-call | tf_op jit(solution)/shard_map/mix/pallas_call | solution.py:442
  135.9 2.1 %copy.8 = bf16[48,8192]{1,0:T(8,128)(2,1)} copy(bf16[48,8192]{1,0:T(8,128)(2,1)} %mix.1) | data formatting | bytes 1572864
Async XLA Ops:
  3.5 37.6 %copy-start.5 = (s32[32]{0:T(128)S(1)}, s32[32]{0:T(128)}, u32[]{:S(2)}) copy-start(s32[32]{0:T(128)} %span.1) | copy-start | bytes 388
  41.1 1.9 %copy-start = (bf16[16,384,256]{2,1,0:T(8,128)(2,1)S(1)}, bf16[16,384,256]{2,1,0:T(8,128)(2,1)}, u32[]{:S(2)}) copy-start(bf16[16,384,256]{2,1,0:T(8,128)(2,1)} %get-tuple-element.10.kv) | copy-start | bytes 9437188
  42.9 1.0 copy-start.2
  43.9 0.8 copy-start.3
  44.7 0.7 copy-start.4
  86.7 0.9 copy-start.1

commit v2 on v1

v2 whole, which is shorter than its diff:
```python
import functools
import math

import jax
import jax.numpy as jnp
from jax import lax
from jax.experimental import pallas as pl
from jax.experimental.pallas import tpu as pltpu
from jax.sharding import PartitionSpec as P

MESH = pl.DeviceIdType.MESH
HEAD = 128
ROWS = 384
HALF = 192
BLOCK = 64
QT = 208
NEG = -1e30
VMEM_BYTES = 60 << 20
LOG2_SCALE = math.log2(math.e) / math.sqrt(HEAD)
F32 = jnp.float32
BF16 = jnp.bfloat16


def coords():
    i = lax.axis_index("ctx")
    j = lax.axis_index("head")
    return j // 2, i // 4, (i // 2) % 2, j % 2, i % 2


def ctx_of(y, zl, c):
    return (y * 2 + zl) * 2 + c


def rcopy(src, dst, ssem, rsem, dev):
    return pltpu.make_async_remote_copy(
        src_ref=src, dst_ref=dst, send_sem=ssem, recv_sem=rsem, device_id=dev, device_id_type=MESH
    )


def greet(devs):
    barrier = pltpu.get_barrier_semaphore()
    for dev in devs:
        pl.semaphore_signal(barrier, inc=1, device_id=dev, device_id_type=MESH)
    return lambda: pl.semaphore_wait(barrier, len(devs))


def kernel(
    span, act, nmask, mvec, w, wo, out,
    lhs, wbuf, st, kv, q, msk, qt, m_ref, o_ref, att, abuf, wown, wp, keep, xs, xr, zs, zr,
    act_l, w_l, wo_l, own_l, f_s, f_r, g_r, q_s, q_r, m_s, m_r, zk_s, zf_s, c_s, a_s, a_r,
    wx_s, wx_r, wc_s, wc_r, wy_s, wy_r, wf_s, wf_r, x_s, x_r, z_s, z_r,
):
    x, y, zl, zh, c = coords()
    hd = lax.axis_index("head")
    me = ctx_of(y, zl, c)
    ys = [y] + [lax.rem(y + k, 4) for k in (1, 2, 3)]
    x2 = lax.rem(x + 2, 4)
    ydev = [(ctx_of(ys[k], zl, c), hd) for k in range(4)]
    adev = [ydev, [(ctx_of(ys[k], zl, c), x2 * 2 + zh) for k in range(4)]]
    zdev = (ctx_of(y, 1 - zl, c), hd)
    ddev = (ctx_of(ys[2], 1 - zl, c), hd)
    cdev = (ctx_of(y, zl, 1 - c), hd)
    xup = (me, lax.rem(x + 1, 4) * 2 + zh)
    xdn = (me, lax.rem(x + 3, 4) * 2 + zh)
    hdev = (me, x * 2 + 1 - zh)
    wydev = (ctx_of(lax.rem(y + 1 + 2 * c, 4), zl, c), hd)
    arrive = greet(ydev[1:] + adev[1] + [zdev, ddev, cdev, xup, xdn, hdev])

    sends = []

    def start(cp):
        cp.start()
        sends.append(cp)

    loads = []
    for kc in range(4):
        part = pl.ds(kc * 1024, 1024)
        pair = (
            pltpu.make_async_copy(act.at[:, part], lhs.at[pl.ds(0, ROWS), part], act_l.at[kc]),
            pltpu.make_async_copy(w.at[0, part], wbuf.at[0, part], w_l.at[kc]),
        )
        for cp in pair:
            cp.start()
        loads.append(pair)
    wk = pltpu.make_async_copy(w.at[1], wbuf.at[1], w_l.at[4])
    wv = pltpu.make_async_copy(w.at[2], wbuf.at[2], w_l.at[5])
    wk.start()
    wv.start()
    qd = lax.rem(y, 2) * 2 + c
    order = (qd, qd + 1 - 2 * c, lax.rem(qd + 2, 4), lax.rem(qd + 2, 4) + 1 - 2 * c)
    wol = []
    for n in range(4):
        col = pl.multiple_of(order[n] * 1024, 1024)
        cp = pltpu.make_async_copy(wo.at[:, pl.ds(col, 1024)], wown.at[n], wo_l.at[n])
        cp.start()
        wol.append(cp)
    lhs[pl.ds(ROWS, 16), :] = jnp.broadcast_to(mvec[...], (16, 4096))
    msk[y] = jnp.broadcast_to(nmask[...].astype(F32), (8, ROWS))

    def keep_heads(m, r):
        for j in range(4):
            st[m, j] = r[:, j * HEAD : (j + 1) * HEAD].astype(BF16)

    rows = pl.ds(0, ROWS)
    r = None
    for kc in range(4):
        for cp in loads[kc]:
            cp.wait()
        part = pl.ds(kc * 1024, 1024)
        d = jnp.dot(lhs[:, part], wbuf[0, part], preferred_element_type=F32)
        r = d if r is None else r + d
    keep_heads(0, r * LOG2_SCALE)
    arrive()
    for k in (1, 3, 2):
        start(rcopy(st.at[0, ys[k], rows], q.at[y], q_s.at[k], q_r.at[y], ydev[k]))
        start(rcopy(msk.at[y], msk.at[y], m_s.at[k], m_r.at[y], ydev[k]))
    q[y] = st[0, y, rows]

    for m, cp in ((1, wk), (2, wv)):
        cp.wait()
        keep_heads(m, jnp.dot(lhs[...], wbuf[m], preferred_element_type=F32))
        dst = kv.at[me, m - 1]
        start(rcopy(st.at[m, y, rows], dst, zk_s.at[m - 1], f_r.at[m - 1, me], zdev))
        for k in (1, 3):
            start(rcopy(st.at[m, ys[k], rows], dst, f_s.at[m - 1, k], f_r.at[m - 1, me], ydev[k]))
        kv[me, m - 1] = st[m, y, rows]
    start(rcopy(kv.at[me], kv.at[me], c_s.at[0], g_r.at[me], cdev))
    for m in (1, 2):
        dst = kv.at[me, m - 1]
        start(rcopy(st.at[m, ys[2], rows], dst, f_s.at[m - 1, 2], f_r.at[m - 1, me], ydev[2]))
        start(rcopy(st.at[m, ys[2], rows], dst, f_s.at[m - 1, 0], f_r.at[m - 1, me], ddev))
    for e in range(2):
        col = pl.multiple_of(qd * 1024 + e * 512, 512)
        half = wp.at[0, :, pl.ds(e * 512, 512)]
        start(rcopy(wo.at[:, pl.ds(col, 512)], half, wx_s.at[e], wx_r.at[e], adev[1][0]))

    def here(k, z, split):
        slot = ctx_of(ys[k], z, c)
        if split:
            for m in range(2):
                rcopy(kv.at[slot, m], kv.at[slot, m], zk_s.at[m], f_r.at[m, slot], cdev).wait_recv()
        else:
            rcopy(kv.at[slot], kv.at[slot], zk_s.at[0], g_r.at[slot], cdev).wait_recv()
        return slot

    def to_core(n, slot):
        start(rcopy(kv.at[slot], kv.at[slot], c_s.at[n], g_r.at[slot], cdev))

    def to_z(n, slot):
        start(rcopy(kv.at[slot], kv.at[slot], zf_s.at[n], g_r.at[slot], zdev))

    def from_core(k, z):
        slot = ctx_of(ys[k], z, 1 - c)
        rcopy(kv.at[slot], kv.at[slot], zk_s.at[0], g_r.at[slot], cdev).wait_recv()

    def send_wp(e):
        half = wp.at[0, :, pl.ds(e * 512, 512)]
        rcopy(half, half, wx_s.at[e], wx_r.at[e], cdev).wait_recv()
        start(rcopy(half, wp.at[1, :, pl.ds(e * 512, 512)], wc_s.at[e], wc_r.at[e], cdev))
        start(rcopy(half, wp.at[2, :, pl.ds(e * 512, 512)], wy_s.at[e], wy_r.at[e], wydev))

    def chunk(pa, pb):
        place = lax.broadcasted_iota(jnp.int32, (1, 4 * ROWS), 1) // HALF
        ks = jnp.zeros((1, 4 * ROWS), jnp.int32)
        for n in range(8):
            ks = jnp.where(place == n, span[4 * (pa if n < 4 else pb) + n % 4], ks)
        refs = [(p, m) for m in range(2) for p in (pa, pb)]
        got = [kv[pl.ds(2 * p, 2), m].reshape(2 * ROWS, HEAD) for p, m in refs]
        k = jnp.concatenate(got[:2], axis=0)
        v = jnp.concatenate(got[2:], axis=0)
        return k, jnp.concatenate([v, jnp.ones((4 * ROWS, HEAD), BF16)], axis=1), ks

    def attend(i, u, keys, first):
        k, v, ks = keys
        sc = lax.dot_general(qt[i], k, (((1,), (1,)), ((), ())), preferred_element_type=F32)
        sc = sc + jnp.where(ks < u, F32(0), F32(NEG))
        top = jnp.max(sc, axis=1, keepdims=True)
        if first:
            new = jnp.maximum(top, F32(NEG))
        else:
            old = m_ref[i][:, :1]
            new = jnp.maximum(old, top)
        p = jnp.exp2(sc - new).astype(BF16)
        o = jnp.dot(p, v, preferred_element_type=F32)
        if not first:
            o = o_ref[i] * jnp.exp2(old - new) + o
        return new, o

    def step(pa, pb, first):
        keys = chunk(pa, pb)
        for i in range(8):
            u = span[2 * ctx_of(i // 2, zl, c) + i % 2]
            new, o = attend(i, u, keys, first)
            m_ref[i] = jnp.broadcast_to(new, (QT, HEAD))
            o_ref[i] = o

    def pair(k, z):
        return ys[k] * 2 + z

    to_core(1, here(0, 1 - zl, True))
    for n, k in ((0, 1), (1, 3)):
        slot = here(k, zl, True)
        to_z(n, slot)
        to_core(2 + n, slot)
    for k in (1, 3, 2):
        rcopy(q.at[ys[k]], q.at[ys[k]], q_s.at[1], q_r.at[ys[k]], cdev).wait_recv()
        rcopy(msk.at[ys[k]], msk.at[ys[k]], m_s.at[1], m_r.at[ys[k]], cdev).wait_recv()
    for s in range(4):
        for h in range(2):
            qt[2 * s + h, pl.ds(0, HALF), :] = q[s, pl.ds(h * HALF, HALF), :]
            qt[2 * s + h, pl.ds(HALF, 16), :] = st[0, y, pl.ds(ROWS, 16), :]
    from_core(0, zl)
    from_core(0, 1 - zl)
    step(pair(0, zl), pair(0, 1 - zl), True)
    from_core(1, zl)
    from_core(3, zl)
    step(pair(1, zl), pair(3, zl), False)
    to_core(4, here(2, zl, True))
    to_core(5, here(1, 1 - zl, False))
    send_wp(0)
    from_core(2, zl)
    from_core(1, 1 - zl)
    step(pair(2, zl), pair(1, 1 - zl), False)
    to_core(6, here(3, 1 - zl, False))
    to_core(7, here(2, 1 - zl, True))
    send_wp(1)
    from_core(3, 1 - zl)
    from_core(2, 1 - zl)

    p_x = x // 2
    km = st[1, y, pl.ds(ROWS, 16), :]
    vm = st[2, y, pl.ds(ROWS, 16), :][:1].astype(F32)
    vm = jnp.concatenate([vm, jnp.ones((1, HEAD), F32)], axis=1)
    rowi = lax.broadcasted_iota(jnp.int32, (QT, HALF), 0)
    coli = lax.broadcasted_iota(jnp.int32, (QT, HALF), 1)
    bi = jnp.where(rowi < HALF, rowi // BLOCK, jnp.minimum(rowi - HALF, 2))
    bj = coli // BLOCK
    last = chunk(pair(3, 1 - zl), pair(2, 1 - zl))

    def finish(s, h):
        i = 2 * s + h
        src = ctx_of(s, zl, c)
        mp, op = attend(i, span[2 * src + h], last, False)
        qi = qt[i]
        ko = kv[src, 0, pl.ds(h * HALF, HALF), :]
        vo = jnp.concatenate([kv[src, 1, pl.ds(h * HALF, HALF), :], jnp.ones((HALF, HEAD), BF16)], axis=1)
        so = lax.dot_general(qi, ko, (((1,), (1,)), ((), ())), preferred_element_type=F32)
        sm = lax.dot_general(qi, km, (((1,), (1,)), ((), ())), preferred_element_type=F32)[:, :1]
        mrow = msk[s, pl.ds(0, 1), pl.ds(h * HALF, HALF)]

        sc = jnp.where(bj <= bi, so, F32(NEG))
        mc = jnp.maximum(mp, jnp.max(sc, axis=1, keepdims=True))
        pc = jnp.where(bj <= bi, jnp.exp2(sc - mc), F32(0)).astype(BF16)
        oc = op * jnp.exp2(mp - mc) + jnp.dot(pc, vo, preferred_element_type=F32)
        clean = (oc[:HALF, :HEAD] / oc[:HALF, HEAD:]).astype(BF16)

        hit = (bj == bi) & (mrow > 0.5)
        sn = jnp.where(hit, sm, sc)
        mn = jnp.maximum(mp, jnp.max(sn, axis=1, keepdims=True))
        pn = jnp.where(bj <= bi, jnp.exp2(sn - mn), F32(0)).astype(BF16)
        pz = jnp.where(hit, F32(0), pn.astype(F32))
        wm = jnp.sum(pn.astype(F32) - pz, axis=1, keepdims=True)
        on = op * jnp.exp2(mp - mn) + jnp.dot(pz.astype(BF16), vo, preferred_element_type=F32) + wm * vm
        an = on[:, :HEAD] / on[:, HEAD:]
        mcol = jnp.sum(jnp.where(rowi == coli, mrow, F32(0)), axis=1, keepdims=True)[:HALF]
        masked = jnp.concatenate(
            [jnp.broadcast_to(an[HALF + b : HALF + b + 1], (BLOCK, HEAD)) for b in range(3)], axis=0
        )
        noisy = jnp.where(mcol > 0.5, masked, an[:HALF]).astype(BF16)

        for b in range(4):
            xo = 2 * h + b // 2
            zo = b % 2
            near = zo == p_x
            side = jnp.where(near, lax.rem(x + 1, 4), lax.rem(x + 3, 4))
            pos = jnp.where(
                xo == x,
                zo,
                jnp.where(xo == x2, 4 + zo, jnp.where(near, 0, 4) + jnp.where(xo == side, 2, 3)),
            )
            att[s, pos, pl.ds(0, 48), :] = clean[b * 48 : (b + 1) * 48]
            att[s, pos, pl.ds(48, 48), :] = noisy[b * 48 : (b + 1) * 48]

    own = None
    for n, k in enumerate((2, 1, 3, 0)):
        s = ys[k]
        finish(s, 0)
        finish(s, 1)
        for t in (1, 0):
            dst = abuf.at[:, :, pl.ds(pl.multiple_of((4 * t + y) * HEAD, HEAD), HEAD)]
            if (t, k) == (0, 0):
                own = pltpu.make_async_copy(att.at[s, pl.ds(0, 4)], dst, own_l)
                own.start()
            else:
                start(rcopy(att.at[s, pl.ds(4 * t, 4)], dst, a_s.at[4 * t + k], a_r.at[4 * t + y], adev[t][k]))
    own.wait()
    for t, k in ((0, 2), (1, 2), (0, 1), (1, 1), (0, 3), (1, 3), (1, 0)):
        slot = 4 * t + ys[k]
        dst = abuf.at[:, :, pl.ds(pl.multiple_of(slot * HEAD, HEAD), HEAD)]
        rcopy(att.at[0, pl.ds(0, 4)], dst, a_s.at[1], a_r.at[slot], cdev).wait_recv()

    def matmul(n):
        j, e = n // 2, n % 2
        if e == 0:
            wol[j].wait()
        cols = pl.ds(e * 512, 512)
        if j == 1:
            half = wp.at[1, :, cols]
            rcopy(half, half, wc_s.at[e], wc_r.at[e], cdev).wait_recv()
        if j == 2:
            half = wp.at[2, :, cols]
            rcopy(half, half, wy_s.at[e], wy_r.at[e], cdev).wait_recv()
            start(rcopy(half, wp.at[3, :, cols], wf_s.at[e], wf_r.at[e], cdev))
        if j == 3:
            half = wp.at[3, :, cols]
            rcopy(half, half, wf_s.at[e], wf_r.at[e], cdev).wait_recv()
        a = abuf[...].reshape(ROWS, 1024)
        r = jnp.dot(a[:, :512], wown[j, :, cols], preferred_element_type=F32)
        r = r + jnp.dot(a[:, 512:], wp[j, :, cols], preferred_element_type=F32)
        keep[n] = r[:192].reshape(2, 96, 512)
        xs[n, 0] = r[192:288].astype(BF16)
        xs[n, 1] = r[288:].astype(BF16)
        start(rcopy(xs.at[n, 0], xr.at[n, 0], x_s.at[n, 0], x_r.at[n, 0], xup))
        start(rcopy(xs.at[n, 1], xr.at[n, 1], x_s.at[n, 1], x_r.at[n, 1], xdn))

    from_below = lax.rem(x + 3, 4) // 2

    def reduce_x(n):
        for d in range(2):
            rcopy(xs.at[n, d], xr.at[n, d], x_s.at[n, d], x_r.at[n, d], xup).wait_recv()
        far = 1 - zh
        keep[n, zh] = keep[n, zh] + xr[n, (zh + from_below) % 2].astype(F32)
        zs[n] = (keep[n, far] + xr[n, (far + from_below) % 2].astype(F32)).astype(BF16)
        start(rcopy(zs.at[n], zr.at[n], z_s.at[n], z_r.at[n], hdev))

    def reduce_z(n):
        rcopy(zs.at[n], zr.at[n], z_s.at[n], z_r.at[n], hdev).wait_recv()
        total = (keep[n, zh] + zr[n].astype(F32)).astype(BF16)
        col = pl.multiple_of(order[n // 2] * 1024 + (n % 2) * 512, 512)
        out[:, pl.ds(col, 512)] = total[:48]
        out[:, pl.ds(4096 + col, 512)] = total[48:]

    for n in range(4):
        matmul(n)
    reduce_x(0)
    reduce_x(1)
    matmul(4)
    reduce_x(2)
    matmul(5)
    reduce_z(0)
    reduce_x(3)
    matmul(6)
    reduce_z(1)
    reduce_x(4)
    matmul(7)
    reduce_z(2)
    reduce_x(5)
    reduce_z(3)
    reduce_x(6)
    reduce_z(4)
    reduce_x(7)
    for n in (5, 6, 7):
        reduce_z(n)
    for cp in sends:
        cp.wait_send()


def vmem():
    return pl.BlockSpec(memory_space=pltpu.VMEM)


def anyspace():
    return pl.BlockSpec(memory_space=pl.ANY)


def shards(activations, noise_mask, span_order, mask_vector, input_weights, output_weight):
    dma = pltpu.SemaphoreType.DMA
    return pl.pallas_call(
        kernel,
        out_shape=jax.ShapeDtypeStruct((48, 8192), BF16),
        in_specs=[pl.BlockSpec(memory_space=pltpu.SMEM), anyspace(), vmem(), vmem(), anyspace(), anyspace()],
        out_specs=vmem(),
        scratch_shapes=[
            pltpu.VMEM((ROWS + 16, 4096), BF16),
            pltpu.VMEM((3, 4096, 512), BF16),
            pltpu.VMEM((3, 4, ROWS + 16, HEAD), BF16),
            pltpu.VMEM((16, 2, ROWS, HEAD), BF16),
            pltpu.VMEM((4, ROWS, HEAD), BF16),
            pltpu.VMEM((4, 8, ROWS), F32),
            pltpu.VMEM((8, QT, HEAD), BF16),
            pltpu.VMEM((8, QT, HEAD), F32),
            pltpu.VMEM((8, QT, 2 * HEAD), F32),
            pltpu.VMEM((4, 8, 96, HEAD), BF16),
            pltpu.VMEM((4, 96, 1024), BF16),
            pltpu.VMEM((4, 512, 1024), BF16),
            pltpu.VMEM((4, 512, 1024), BF16),
            pltpu.VMEM((8, 2, 96, 512), F32),
            pltpu.VMEM((8, 2, 96, 512), BF16),
            pltpu.VMEM((8, 2, 96, 512), BF16),
            pltpu.VMEM((8, 96, 512), BF16),
            pltpu.VMEM((8, 96, 512), BF16),
            dma((4,)),
            dma((6,)),
            dma((4,)),
            dma,
            dma((2, 4)),
            dma((2, 16)),
            dma((16,)),
            dma((4,)),
            dma((4,)),
            dma((4,)),
            dma((4,)),
            dma((2,)),
            dma((2,)),
            dma((8,)),
            dma((8,)),
            dma((8,)),
            dma((2,)),
            dma((2,)),
            dma((2,)),
            dma((2,)),
            dma((2,)),
            dma((2,)),
            dma((2,)),
            dma((2,)),
            dma((8, 2)),
            dma((8, 2)),
            dma((8,)),
            dma((8,)),
        ],
        compiler_params=pltpu.CompilerParams(
            collective_id=1, has_side_effects=True, vmem_limit_bytes=VMEM_BYTES
        ),
        name="whole",
    )(
        span_order,
        activations,
        noise_mask.reshape(1, ROWS),
        mask_vector.reshape(1, 4096),
        input_weights,
        output_weight,
    )


def solution(mesh):
    in_specs = (P("ctx", None), P("ctx"), P(), P(), P(None, None, "head"), P("head", None))
    out_specs = P(("ctx", "head"), None)
    return jax.shard_map(shards, mesh=mesh, in_specs=in_specs, out_specs=out_specs, check_vma=False)
```

time: 138 us -> 87.6 us (0.63)
  Pallas kernels: 127 us -> 82.7 us
  local copies, waits for them, and re-layouts: 10.8 us -> 4.63 us
    pallas_call x3 -> x1, Pallas kernels: 127 us -> 82.7 us  [shards(): pl.pallas_call(kernel, out_shape=jax.ShapeDtypeStruct((48, 8192), BF16),...]
    unnamed x13 -> x1, local copies, waits for them, and re-layouts: 7.33 us -> 2.06 us
where the time goes in v2:
time: 87.6 us; the launch traced here: 87.4 us
  Pallas kernels  82.7 us (94%)
  local copies, waits for them, and re-layouts  4.63 us (5%)
    pallas_call x1, Pallas kernels, shards(): pl.pallas_call(kernel, out_shape=jax.ShapeDtypeStruct((48, 8192), BF16),...  82.7 us
    unnamed x1, local copies, waits for them, and re-layouts  2.06 us

profile of v2, /device:TPU:0, one launch (start us, length us, event | category | flops | bytes accessed | tf_op | source)
XLA Modules:
  0.0 87.4 jit_solution(15119335798588375004)
XLA Ops:
  0.0 1.3 %reshape.6.nmask = s32[1,384]{1,0:T(1,128)} reshape(s32[384]{0:T(512)} %param.7) | data formatting | bytes 3072 | tf_op jit(solution)/shard_map/reshape | solution.py:438
  1.3 1.3 %reshape.7.mvec = bf16[1,4096]{1,0:T(2,128)(2,1)} reshape(bf16[4096]{0:T(1024)(128)(2,1)} %param.9) | data formatting | bytes 16384 | tf_op jit(solution)/shard_map/reshape | solution.py:439
  2.6 82.7 %whole.1 = bf16[48,8192]{1,0:T(8,128)(2,1)} custom-call(s32[32]{0:T(128)} %span.1, bf16[384,4096]{1,0:T(8,128)(2,1)} %act.1, s32[1,384]{1,0:T(1,128)} %reshape.6.nmask, bf16[1,4096]{1,0:T(2,128)(2,1)} %reshape.7.mvec, bf16[3,4096,512]{2,1,0:T(8,128)(2,1)} %w.1, bf16[512,4096]{1,0:T(8,128)(2,1)} %wo.1), custom_call_target="tpu_custom_call" | custom-call | tf_op jit(solution)/shard_map/whole/pallas_call | solution.py:378
  85.3 2.1 %copy.8 = bf16[48,8192]{1,0:T(8,128)(2,1)} copy(bf16[48,8192]{1,0:T(8,128)(2,1)} %whole.1) | data formatting | bytes 1572864

commit v3 on v2

--- a/solution.py
+++ b/solution.py
@@ -16,6 +16,7 @@
 QT = 208
 NEG = -1e30
 VMEM_BYTES = 60 << 20
+NC = 256
 LOG2_SCALE = math.log2(math.e) / math.sqrt(HEAD)
 F32 = jnp.float32
 BF16 = jnp.bfloat16
@@ -75,42 +76,53 @@
     loads = []
     for kc in range(4):
         part = pl.ds(kc * 1024, 1024)
-        pair = (
-            pltpu.make_async_copy(act.at[:, part], lhs.at[pl.ds(0, ROWS), part], act_l.at[kc]),
-            pltpu.make_async_copy(w.at[0, part], wbuf.at[0, part], w_l.at[kc]),
+        loads.append(
+            (
+                pltpu.make_async_copy(act.at[:, part], lhs.at[pl.ds(0, ROWS), part], act_l.at[kc]),
+                pltpu.make_async_copy(w.at[0, part], wbuf.at[0, part], w_l.at[kc]),
+            )
         )
-        for cp in pair:
-            cp.start()
-        loads.append(pair)
     wk = pltpu.make_async_copy(w.at[1], wbuf.at[1], w_l.at[4])
     wv = pltpu.make_async_copy(w.at[2], wbuf.at[2], w_l.at[5])
-    wk.start()
-    wv.start()
     qd = lax.rem(y, 2) * 2 + c
     order = (qd, qd + 1 - 2 * c, lax.rem(qd + 2, 4), lax.rem(qd + 2, 4) + 1 - 2 * c)
     wol = []
     for n in range(4):
         col = pl.multiple_of(order[n] * 1024, 1024)
-        cp = pltpu.make_async_copy(wo.at[:, pl.ds(col, 1024)], wown.at[n], wo_l.at[n])
-        cp.start()
-        wol.append(cp)
-    lhs[pl.ds(ROWS, 16), :] = jnp.broadcast_to(mvec[...], (16, 4096))
-    msk[y] = jnp.broadcast_to(nmask[...].astype(F32), (8, ROWS))
+        wol.append(pltpu.make_async_copy(wo.at[:, pl.ds(col, 1024)], wown.at[n], wo_l.at[n]))
+
+    def load(*copies):
+        for cp in copies:
+            cp.start()
+
+    load(*loads[0], *loads[1], *loads[2])
+    lhs[pl.ds(ROWS, 16), :] = jnp.broadcast_to(mvec[...].reshape(1, 4096), (16, 4096))
+    msk[y] = jnp.broadcast_to(nmask[...].astype(F32).reshape(1, ROWS), (8, ROWS))
 
     def keep_heads(m, r):
         for j in range(4):
             st[m, j] = r[:, j * HEAD : (j + 1) * HEAD].astype(BF16)
+
+    arrive()
+    for e in range(2):
+        col = pl.multiple_of(qd * 1024 + e * 512, 512)
+        half = wp.at[0, :, pl.ds(e * 512, 512)]
+        start(rcopy(wo.at[:, pl.ds(col, 512)], half, wx_s.at[e], wx_r.at[e], adev[1][0]))
 
     rows = pl.ds(0, ROWS)
     r = None
     for kc in range(4):
         for cp in loads[kc]:
             cp.wait()
+        if kc == 0:
+            load(*loads[3])
+        if kc == 1:
+            load(wk)
         part = pl.ds(kc * 1024, 1024)
         d = jnp.dot(lhs[:, part], wbuf[0, part], preferred_element_type=F32)
         r = d if r is None else r + d
+    load(wv)
     keep_heads(0, r * LOG2_SCALE)
-    arrive()
     for k in (1, 3, 2):
         start(rcopy(st.at[0, ys[k], rows], q.at[y], q_s.at[k], q_r.at[y], ydev[k]))
         start(rcopy(msk.at[y], msk.at[y], m_s.at[k], m_r.at[y], ydev[k]))
@@ -118,6 +130,8 @@
 
     for m, cp in ((1, wk), (2, wv)):
         cp.wait()
+        if m == 2:
+            load(*wol)
         keep_heads(m, jnp.dot(lhs[...], wbuf[m], preferred_element_type=F32))
         dst = kv.at[me, m - 1]
         start(rcopy(st.at[m, y, rows], dst, zk_s.at[m - 1], f_r.at[m - 1, me], zdev))
@@ -129,11 +143,6 @@
         dst = kv.at[me, m - 1]
         start(rcopy(st.at[m, ys[2], rows], dst, f_s.at[m - 1, 2], f_r.at[m - 1, me], ydev[2]))
         start(rcopy(st.at[m, ys[2], rows], dst, f_s.at[m - 1, 0], f_r.at[m - 1, me], ddev))
-    for e in range(2):
-        col = pl.multiple_of(qd * 1024 + e * 512, 512)
-        half = wp.at[0, :, pl.ds(e * 512, 512)]
-        start(rcopy(wo.at[:, pl.ds(col, 512)], half, wx_s.at[e], wx_r.at[e], adev[1][0]))
-
     def here(k, z, split):
         slot = ctx_of(ys[k], z, c)
         if split:
@@ -212,12 +221,12 @@
     from_core(0, zl)
     from_core(0, 1 - zl)
     step(pair(0, zl), pair(0, 1 - zl), True)
+    send_wp(0)
     from_core(1, zl)
     from_core(3, zl)
     step(pair(1, zl), pair(3, zl), False)
     to_core(4, here(2, zl, True))
     to_core(5, here(1, 1 - zl, False))
-    send_wp(0)
     from_core(2, zl)
     from_core(1, 1 - zl)
     step(pair(2, zl), pair(1, 1 - zl), False)
@@ -300,24 +309,22 @@
         rcopy(att.at[0, pl.ds(0, 4)], dst, a_s.at[1], a_r.at[slot], cdev).wait_recv()
 
     def matmul(n):
-        j, e = n // 2, n % 2
-        if e == 0:
+        j, e = n // 4, n // 2 % 2
+        if n % 4 == 0:
             wol[j].wait()
-        cols = pl.ds(e * 512, 512)
-        if j == 1:
-            half = wp.at[1, :, cols]
+        half = wp.at[j, :, pl.ds(e * 512, 512)]
+        if n % 2 == 0 and j == 1:
             rcopy(half, half, wc_s.at[e], wc_r.at[e], cdev).wait_recv()
-        if j == 2:
-            half = wp.at[2, :, cols]
+        if n % 2 == 0 and j == 2:
             rcopy(half, half, wy_s.at[e], wy_r.at[e], cdev).wait_recv()
-            start(rcopy(half, wp.at[3, :, cols], wf_s.at[e], wf_r.at[e], cdev))
-        if j == 3:
-            half = wp.at[3, :, cols]
+            start(rcopy(half, wp.at[3, :, pl.ds(e * 512, 512)], wf_s.at[e], wf_r.at[e], cdev))
+        if n % 2 == 0 and j == 3:
             rcopy(half, half, wf_s.at[e], wf_r.at[e], cdev).wait_recv()
+        cols = pl.ds(n % 4 * NC, NC)
         a = abuf[...].reshape(ROWS, 1024)
         r = jnp.dot(a[:, :512], wown[j, :, cols], preferred_element_type=F32)
         r = r + jnp.dot(a[:, 512:], wp[j, :, cols], preferred_element_type=F32)
-        keep[n] = r[:192].reshape(2, 96, 512)
+        keep[n] = r[:192].reshape(2, 96, NC)
         xs[n, 0] = r[192:288].astype(BF16)
         xs[n, 1] = r[288:].astype(BF16)
         start(rcopy(xs.at[n, 0], xr.at[n, 0], x_s.at[n, 0], x_r.at[n, 0], xup))
@@ -336,30 +343,19 @@
     def reduce_z(n):
         rcopy(zs.at[n], zr.at[n], z_s.at[n], z_r.at[n], hdev).wait_recv()
         total = (keep[n, zh] + zr[n].astype(F32)).astype(BF16)
-        col = pl.multiple_of(order[n // 2] * 1024 + (n % 2) * 512, 512)
-        out[:, pl.ds(col, 512)] = total[:48]
-        out[:, pl.ds(4096 + col, 512)] = total[48:]
+        col = pl.multiple_of(order[n // 4] * 1024 + n % 4 * NC, NC)
+        out[:, pl.ds(col, NC)] = total[:48]
+        out[:, pl.ds(4096 + col, NC)] = total[48:]
 
     for n in range(4):
         matmul(n)
-    reduce_x(0)
-    reduce_x(1)
-    matmul(4)
-    reduce_x(2)
-    matmul(5)
-    reduce_z(0)
-    reduce_x(3)
-    matmul(6)
-    reduce_z(1)
-    reduce_x(4)
-    matmul(7)
-    reduce_z(2)
-    reduce_x(5)
-    reduce_z(3)
-    reduce_x(6)
-    reduce_z(4)
-    reduce_x(7)
-    for n in (5, 6, 7):
+    for n in range(16):
+        reduce_x(n)
+        if n + 4 < 16:
+            matmul(n + 4)
+        if n >= 3:
+            reduce_z(n - 3)
+    for n in (13, 14, 15):
         reduce_z(n)
     for cp in sends:
         cp.wait_send()
@@ -394,11 +390,11 @@
             pltpu.VMEM((4, 96, 1024), BF16),
             pltpu.VMEM((4, 512, 1024), BF16),
             pltpu.VMEM((4, 512, 1024), BF16),
-            pltpu.VMEM((8, 2, 96, 512), F32),
-            pltpu.VMEM((8, 2, 96, 512), BF16),
-            pltpu.VMEM((8, 2, 96, 512), BF16),
-            pltpu.VMEM((8, 96, 512), BF16),
-            pltpu.VMEM((8, 96, 512), BF16),
+            pltpu.VMEM((16, 2, 96, NC), F32),
+            pltpu.VMEM((16, 2, 96, NC), BF16),
+            pltpu.VMEM((16, 2, 96, NC), BF16),
+            pltpu.VMEM((16, 96, NC), BF16),
+            pltpu.VMEM((16, 96, NC), BF16),
             dma((4,)),
             dma((6,)),
             dma((4,)),
@@ -423,10 +419,10 @@
             dma((2,)),
             dma((2,)),
             dma((2,)),
-            dma((8, 2)),
-            dma((8, 2)),
-            dma((8,)),
-            dma((8,)),
+            dma((16, 2)),
+            dma((16, 2)),
+            dma((16,)),
+            dma((16,)),
         ],
         compiler_params=pltpu.CompilerParams(
             collective_id=1, has_side_effects=True, vmem_limit_bytes=VMEM_BYTES
@@ -435,8 +431,8 @@
     )(
         span_order,
         activations,
-        noise_mask.reshape(1, ROWS),
-        mask_vector.reshape(1, 4096),
+        noise_mask,
+        mask_vector,
         input_weights,
         output_weight,
     )

time: 87.6 us -> 85.3 us (0.974)
  local copies, waits for them, and re-layouts: 4.63 us -> 2.06 us
    reshape x2 -> x0, local copies, waits for them, and re-layouts: 2.57 us -> none  [the longest x1 1.31 us: shards(): mask_vector.reshape(1, 4096)]
where the time goes in v3:
time: 85.3 us; the launch traced here: 85.1 us
  Pallas kernels  83 us (97%)
  local copies, waits for them, and re-layouts  2.06 us (2%)
    pallas_call x1, Pallas kernels, shards(): pl.pallas_call(kernel, out_shape=jax.ShapeDtypeStruct((48, 8192), BF16),...  83 us
    unnamed x1, local copies, waits for them, and re-layouts  2.06 us

profile of v3, /device:TPU:0, one launch (start us, length us, event | category | flops | bytes accessed | tf_op | source)
XLA Modules:
  0.0 85.1 jit_solution(1437076997650124019)
XLA Ops:
  0.0 83.0 %whole.1 = bf16[48,8192]{1,0:T(8,128)(2,1)} custom-call(s32[32]{0:T(128)} %span.1, bf16[384,4096]{1,0:T(8,128)(2,1)} %act.1, s32[384]{0:T(512)} %nmask.1, bf16[4096]{0:T(1024)(128)(2,1)} %mvec.1, bf16[3,4096,512]{2,1,0:T(8,128)(2,1)} %w.1, bf16[512,4096]{1,0:T(8,128)(2,1)} %wo.1), custom_call_target="tpu_custom_call" | custom-call | tf_op jit(solution)/shard_map/whole/pallas_call | solution.py:374
  83.0 2.1 %copy.8 = bf16[48,8192]{1,0:T(8,128)(2,1)} copy(bf16[48,8192]{1,0:T(8,128)(2,1)} %whole.1) | data formatting | bytes 1572864

commit v4 on v3

--- a/solution.py
+++ b/solution.py
@@ -139,10 +139,6 @@
             start(rcopy(st.at[m, ys[k], rows], dst, f_s.at[m - 1, k], f_r.at[m - 1, me], ydev[k]))
         kv[me, m - 1] = st[m, y, rows]
     start(rcopy(kv.at[me], kv.at[me], c_s.at[0], g_r.at[me], cdev))
-    for m in (1, 2):
-        dst = kv.at[me, m - 1]
-        start(rcopy(st.at[m, ys[2], rows], dst, f_s.at[m - 1, 2], f_r.at[m - 1, me], ydev[2]))
-        start(rcopy(st.at[m, ys[2], rows], dst, f_s.at[m - 1, 0], f_r.at[m - 1, me], ddev))
     def here(k, z, split):
         slot = ctx_of(ys[k], z, c)
         if split:
@@ -211,6 +207,10 @@
         slot = here(k, zl, True)
         to_z(n, slot)
         to_core(2 + n, slot)
+    for m in (1, 2):
+        dst = kv.at[me, m - 1]
+        start(rcopy(st.at[m, ys[2], rows], dst, f_s.at[m - 1, 2], f_r.at[m - 1, me], ydev[2]))
+        start(rcopy(st.at[m, ys[2], rows], dst, f_s.at[m - 1, 0], f_r.at[m - 1, me], ddev))
     for k in (1, 3, 2):
         rcopy(q.at[ys[k]], q.at[ys[k]], q_s.at[1], q_r.at[ys[k]], cdev).wait_recv()
         rcopy(msk.at[ys[k]], msk.at[ys[k]], m_s.at[1], m_r.at[ys[k]], cdev).wait_recv()
@@ -221,12 +221,12 @@
     from_core(0, zl)
     from_core(0, 1 - zl)
     step(pair(0, zl), pair(0, 1 - zl), True)
-    send_wp(0)
     from_core(1, zl)
     from_core(3, zl)
     step(pair(1, zl), pair(3, zl), False)
     to_core(4, here(2, zl, True))
     to_core(5, here(1, 1 - zl, False))
+    send_wp(0)
     from_core(2, zl)
     from_core(1, 1 - zl)
     step(pair(2, zl), pair(1, 1 - zl), False)

time: 85.3 us -> 86.6 us (1.015)
  Pallas kernels: 83 us -> 84.3 us
    pallas_call x1, Pallas kernels: 83 us -> 84.3 us  [shards(): pl.pallas_call(kernel, out_shape=jax.ShapeDtypeStruct((48, 8192), BF16),...]
where the time goes in v4:
time: 86.6 us; the launch traced here: 86.4 us
  Pallas kernels  84.3 us (97%)
  local copies, waits for them, and re-layouts  2.06 us (2%)
    pallas_call x1, Pallas kernels, shards(): pl.pallas_call(kernel, out_shape=jax.ShapeDtypeStruct((48, 8192), BF16),...  84.3 us
    unnamed x1, local copies, waits for them, and re-layouts  2.06 us

profile of v4, /device:TPU:0, one launch (start us, length us, event | category | flops | bytes accessed | tf_op | source)
XLA Modules:
  0.0 86.4 jit_solution(10537585941502417738)
XLA Ops:
  0.0 84.3 %whole.1 = bf16[48,8192]{1,0:T(8,128)(2,1)} custom-call(s32[32]{0:T(128)} %span.1, bf16[384,4096]{1,0:T(8,128)(2,1)} %act.1, s32[384]{0:T(512)} %nmask.1, bf16[4096]{0:T(1024)(128)(2,1)} %mvec.1, bf16[3,4096,512]{2,1,0:T(8,128)(2,1)} %w.1, bf16[512,4096]{1,0:T(8,128)(2,1)} %wo.1), custom_call_target="tpu_custom_call" | custom-call | tf_op jit(solution)/shard_map/whole/pallas_call | solution.py:374
  84.3 2.1 %copy.8 = bf16[48,8192]{1,0:T(8,128)(2,1)} copy(bf16[48,8192]{1,0:T(8,128)(2,1)} %whole.1) | data formatting | bytes 1572864

commit v5 on v4

--- a/solution.py
+++ b/solution.py
@@ -47,7 +47,7 @@
 
 def kernel(
     span, act, nmask, mvec, w, wo, out,
-    lhs, wbuf, st, kv, q, msk, qt, m_ref, o_ref, att, abuf, wown, wp, keep, xs, xr, zs, zr,
+    lhs, wbuf, st, kv, q, msk, qt, m_ref, o_ref, mc_ref, oc_ref, mn_ref, on_ref, att, abuf, wown, wp, keep, xs, xr, zs, zr,
     act_l, w_l, wo_l, own_l, f_s, f_r, g_r, q_s, q_r, m_s, m_r, zk_s, zf_s, c_s, a_s, a_r,
     wx_s, wx_r, wc_s, wc_r, wy_s, wy_r, wf_s, wf_r, x_s, x_r, z_s, z_r,
 ):
@@ -202,6 +202,44 @@
     def pair(k, z):
         return ys[k] * 2 + z
 
+    p_x = x // 2
+    rowi = lax.broadcasted_iota(jnp.int32, (QT, HALF), 0)
+    coli = lax.broadcasted_iota(jnp.int32, (QT, HALF), 1)
+    bi = jnp.where(rowi < HALF, rowi // BLOCK, jnp.minimum(rowi - HALF, 2))
+    bj = coli // BLOCK
+
+    def own_keys(s):
+        km = st[1, y, pl.ds(ROWS, 16), :]
+        vm = st[2, y, pl.ds(ROWS, 16), :][:1].astype(F32)
+        vm = jnp.concatenate([vm, jnp.ones((1, HEAD), F32)], axis=1)
+        src = ctx_of(s, zl, c)
+        for h in range(2):
+            i = 2 * s + h
+            qi = jnp.concatenate([q[s, pl.ds(h * HALF, HALF), :], st[0, y, pl.ds(ROWS, 16), :]], axis=0)
+            ko = kv[src, 0, pl.ds(h * HALF, HALF), :]
+            vo = kv[src, 1, pl.ds(h * HALF, HALF), :]
+            vo = jnp.concatenate([vo, jnp.ones((HALF, HEAD), BF16)], axis=1)
+            so = lax.dot_general(qi, ko, (((1,), (1,)), ((), ())), preferred_element_type=F32)
+            sm = lax.dot_general(qi, km, (((1,), (1,)), ((), ())), preferred_element_type=F32)[:, :1]
+            mrow = msk[s, pl.ds(0, 1), pl.ds(h * HALF, HALF)]
+            sc = jnp.where(bj <= bi, so, F32(NEG))
+            mc = jnp.max(sc, axis=1, keepdims=True)
+            pc = jnp.exp2(sc - mc).astype(BF16)
+            mc_ref[i] = jnp.broadcast_to(mc, (QT, HEAD))
+            oc_ref[i] = jnp.dot(pc, vo, preferred_element_type=F32)
+            hit = (bj == bi) & (mrow > 0.5)
+            sn = jnp.where(hit, sm, sc)
+            mn = jnp.max(sn, axis=1, keepdims=True)
+            pn = jnp.exp2(sn - mn).astype(BF16).astype(F32)
+            pz = jnp.where(hit, F32(0), pn)
+            wm = jnp.sum(pn - pz, axis=1, keepdims=True)
+            mn_ref[i] = jnp.broadcast_to(mn, (QT, HEAD))
+            on_ref[i] = jnp.dot(pz.astype(BF16), vo, preferred_element_type=F32) + wm * vm
+
+    for h in range(2):
+        qt[2 * y + h, pl.ds(0, HALF), :] = q[y, pl.ds(h * HALF, HALF), :]
+        qt[2 * y + h, pl.ds(HALF, 16), :] = st[0, y, pl.ds(ROWS, 16), :]
+    own_keys(y)
     to_core(1, here(0, 1 - zl, True))
     for n, k in ((0, 1), (1, 3)):
         slot = here(k, zl, True)
@@ -214,19 +252,22 @@
     for k in (1, 3, 2):
         rcopy(q.at[ys[k]], q.at[ys[k]], q_s.at[1], q_r.at[ys[k]], cdev).wait_recv()
         rcopy(msk.at[ys[k]], msk.at[ys[k]], m_s.at[1], m_r.at[ys[k]], cdev).wait_recv()
-    for s in range(4):
+    for k in (1, 3, 2):
         for h in range(2):
-            qt[2 * s + h, pl.ds(0, HALF), :] = q[s, pl.ds(h * HALF, HALF), :]
-            qt[2 * s + h, pl.ds(HALF, 16), :] = st[0, y, pl.ds(ROWS, 16), :]
+            qt[2 * ys[k] + h, pl.ds(0, HALF), :] = q[ys[k], pl.ds(h * HALF, HALF), :]
+            qt[2 * ys[k] + h, pl.ds(HALF, 16), :] = st[0, y, pl.ds(ROWS, 16), :]
     from_core(0, zl)
     from_core(0, 1 - zl)
     step(pair(0, zl), pair(0, 1 - zl), True)
+    own_keys(ys[1])
+    own_keys(ys[3])
     from_core(1, zl)
     from_core(3, zl)
     step(pair(1, zl), pair(3, zl), False)
     to_core(4, here(2, zl, True))
     to_core(5, here(1, 1 - zl, False))
     send_wp(0)
+    own_keys(ys[2])
     from_core(2, zl)
     from_core(1, 1 - zl)
     step(pair(2, zl), pair(1, 1 - zl), False)
@@ -236,41 +277,16 @@
     from_core(3, 1 - zl)
     from_core(2, 1 - zl)
 
-    p_x = x // 2
-    km = st[1, y, pl.ds(ROWS, 16), :]
-    vm = st[2, y, pl.ds(ROWS, 16), :][:1].astype(F32)
-    vm = jnp.concatenate([vm, jnp.ones((1, HEAD), F32)], axis=1)
-    rowi = lax.broadcasted_iota(jnp.int32, (QT, HALF), 0)
-    coli = lax.broadcasted_iota(jnp.int32, (QT, HALF), 1)
-    bi = jnp.where(rowi < HALF, rowi // BLOCK, jnp.minimum(rowi - HALF, 2))
-    bj = coli // BLOCK
-    last = chunk(pair(3, 1 - zl), pair(2, 1 - zl))
-
-    def finish(s, h):
+    def join(mp, op, mo, oo):
+        top = jnp.maximum(mp, mo)
+        o = op * jnp.exp2(mp - top) + oo * jnp.exp2(mo - top)
+        return o[:, :HEAD] / o[:, HEAD:]
+
+    def finish(s, h, mp, op):
         i = 2 * s + h
-        src = ctx_of(s, zl, c)
-        mp, op = attend(i, span[2 * src + h], last, False)
-        qi = qt[i]
-        ko = kv[src, 0, pl.ds(h * HALF, HALF), :]
-        vo = jnp.concatenate([kv[src, 1, pl.ds(h * HALF, HALF), :], jnp.ones((HALF, HEAD), BF16)], axis=1)
-        so = lax.dot_general(qi, ko, (((1,), (1,)), ((), ())), preferred_element_type=F32)
-        sm = lax.dot_general(qi, km, (((1,), (1,)), ((), ())), preferred_element_type=F32)[:, :1]
         mrow = msk[s, pl.ds(0, 1), pl.ds(h * HALF, HALF)]
-
-        sc = jnp.where(bj <= bi, so, F32(NEG))
-        mc = jnp.maximum(mp, jnp.max(sc, axis=1, keepdims=True))
-        pc = jnp.where(bj <= bi, jnp.exp2(sc - mc), F32(0)).astype(BF16)
-        oc = op * jnp.exp2(mp - mc) + jnp.dot(pc, vo, preferred_element_type=F32)
-        clean = (oc[:HALF, :HEAD] / oc[:HALF, HEAD:]).astype(BF16)
-
-        hit = (bj == bi) & (mrow > 0.5)
-        sn = jnp.where(hit, sm, sc)
-        mn = jnp.maximum(mp, jnp.max(sn, axis=1, keepdims=True))
-        pn = jnp.where(bj <= bi, jnp.exp2(sn - mn), F32(0)).astype(BF16)
-        pz = jnp.where(hit, F32(0), pn.astype(F32))
-        wm = jnp.sum(pn.astype(F32) - pz, axis=1, keepdims=True)
-        on = op * jnp.exp2(mp - mn) + jnp.dot(pz.astype(BF16), vo, preferred_element_type=F32) + wm * vm
-        an = on[:, :HEAD] / on[:, HEAD:]
+        clean = join(mp, op, mc_ref[i][:, :1], oc_ref[i])[:HALF].astype(BF16)
+        an = join(mp, op, mn_ref[i][:, :1], on_ref[i])
         mcol = jnp.sum(jnp.where(rowi == coli, mrow, F32(0)), axis=1, keepdims=True)[:HALF]
         masked = jnp.concatenate(
             [jnp.broadcast_to(an[HALF + b : HALF + b + 1], (BLOCK, HEAD)) for b in range(3)], axis=0
@@ -290,18 +306,26 @@
             att[s, pos, pl.ds(0, 48), :] = clean[b * 48 : (b + 1) * 48]
             att[s, pos, pl.ds(48, 48), :] = noisy[b * 48 : (b + 1) * 48]
 
+    last = chunk(pair(3, 1 - zl), pair(2, 1 - zl))
     own = None
-    for n, k in enumerate((2, 1, 3, 0)):
-        s = ys[k]
-        finish(s, 0)
-        finish(s, 1)
-        for t in (1, 0):
-            dst = abuf.at[:, :, pl.ds(pl.multiple_of((4 * t + y) * HEAD, HEAD), HEAD)]
-            if (t, k) == (0, 0):
-                own = pltpu.make_async_copy(att.at[s, pl.ds(0, 4)], dst, own_l)
-                own.start()
-            else:
-                start(rcopy(att.at[s, pl.ds(4 * t, 4)], dst, a_s.at[4 * t + k], a_r.at[4 * t + y], adev[t][k]))
+    for group in ((2, 1), (3, 0)):
+        done = [
+            [attend(2 * ys[k] + h, span[2 * ctx_of(ys[k], zl, c) + h], last, False) for h in range(2)]
+            for k in group
+        ]
+        for k, parts in zip(group, done):
+            s = ys[k]
+            for h in range(2):
+                finish(s, h, *parts[h])
+            for t in (1, 0):
+                dst = abuf.at[:, :, pl.ds(pl.multiple_of((4 * t + y) * HEAD, HEAD), HEAD)]
+                if (t, k) == (0, 0):
+                    own = pltpu.make_async_copy(att.at[s, pl.ds(0, 4)], dst, own_l)
+                    own.start()
+                else:
+                    start(
+                        rcopy(att.at[s, pl.ds(4 * t, 4)], dst, a_s.at[4 * t + k], a_r.at[4 * t + y], adev[t][k])
+                    )
     own.wait()
     for t, k in ((0, 2), (1, 2), (0, 1), (1, 1), (0, 3), (1, 3), (1, 0)):
         slot = 4 * t + ys[k]
@@ -386,6 +410,10 @@
             pltpu.VMEM((8, QT, HEAD), BF16),
             pltpu.VMEM((8, QT, HEAD), F32),
             pltpu.VMEM((8, QT, 2 * HEAD), F32),
+            pltpu.VMEM((8, QT, HEAD), F32),
+            pltpu.VMEM((8, QT, 2 * HEAD), F32),
+            pltpu.VMEM((8, QT, HEAD), F32),
+            pltpu.VMEM((8, QT, 2 * HEAD), F32),
             pltpu.VMEM((4, 8, 96, HEAD), BF16),
             pltpu.VMEM((4, 96, 1024), BF16),
             pltpu.VMEM((4, 512, 1024), BF16),

time: 86.6 us -> 86.9 us (level)
  no operation moved by 1% of the time
where the time goes in v5:
time: 86.9 us; the launch traced here: 86.7 us
  Pallas kernels  84.6 us (97%)
  local copies, waits for them, and re-layouts  2.06 us (2%)
    pallas_call x1, Pallas kernels, shards(): pl.pallas_call(kernel, out_shape=jax.ShapeDtypeStruct((48, 8192), BF16),...  84.6 us
    unnamed x1, local copies, waits for them, and re-layouts  2.06 us

profile of v5, /device:TPU:0, one launch (start us, length us, event | category | flops | bytes accessed | tf_op | source)
XLA Modules:
  0.0 86.7 jit_solution(12741711201910027605)
XLA Ops:
  0.0 84.6 %whole.1 = bf16[48,8192]{1,0:T(8,128)(2,1)} custom-call(s32[32]{0:T(128)} %span.1, bf16[384,4096]{1,0:T(8,128)(2,1)} %act.1, s32[384]{0:T(512)} %nmask.1, bf16[4096]{0:T(1024)(128)(2,1)} %mvec.1, bf16[3,4096,512]{2,1,0:T(8,128)(2,1)} %w.1, bf16[512,4096]{1,0:T(8,128)(2,1)} %wo.1), custom_call_target="tpu_custom_call" | custom-call | tf_op jit(solution)/shard_map/whole/pallas_call | solution.py:398
  84.6 2.1 %copy.8 = bf16[48,8192]{1,0:T(8,128)(2,1)} copy(bf16[48,8192]{1,0:T(8,128)(2,1)} %whole.1) | data formatting | bytes 1572864

commit v6 on v5

--- a/solution.py
+++ b/solution.py
@@ -15,7 +15,7 @@
 BLOCK = 64
 QT = 208
 NEG = -1e30
-VMEM_BYTES = 60 << 20
+VMEM_BYTES = 52 << 20
 NC = 256
 LOG2_SCALE = math.log2(math.e) / math.sqrt(HEAD)
 F32 = jnp.float32
@@ -139,6 +139,9 @@
             start(rcopy(st.at[m, ys[k], rows], dst, f_s.at[m - 1, k], f_r.at[m - 1, me], ydev[k]))
         kv[me, m - 1] = st[m, y, rows]
     start(rcopy(kv.at[me], kv.at[me], c_s.at[0], g_r.at[me], cdev))
+    for m in (1, 2):
+        dst = kv.at[me, m - 1]
+        start(rcopy(st.at[m, ys[2], rows], dst, f_s.at[m - 1, 2], f_r.at[m - 1, me], ydev[2]))
     def here(k, z, split):
         slot = ctx_of(ys[k], z, c)
         if split:
@@ -247,7 +250,6 @@
         to_core(2 + n, slot)
     for m in (1, 2):
         dst = kv.at[me, m - 1]
-        start(rcopy(st.at[m, ys[2], rows], dst, f_s.at[m - 1, 2], f_r.at[m - 1, me], ydev[2]))
         start(rcopy(st.at[m, ys[2], rows], dst, f_s.at[m - 1, 0], f_r.at[m - 1, me], ddev))
     for k in (1, 3, 2):
         rcopy(q.at[ys[k]], q.at[ys[k]], q_s.at[1], q_r.at[ys[k]], cdev).wait_recv()
@@ -266,14 +268,12 @@
     step(pair(1, zl), pair(3, zl), False)
     to_core(4, here(2, zl, True))
     to_core(5, here(1, 1 - zl, False))
-    send_wp(0)
     own_keys(ys[2])
     from_core(2, zl)
     from_core(1, 1 - zl)
     step(pair(2, zl), pair(1, 1 - zl), False)
     to_core(6, here(3, 1 - zl, False))
     to_core(7, here(2, 1 - zl, True))
-    send_wp(1)
     from_core(3, 1 - zl)
     from_core(2, 1 - zl)
 
@@ -306,6 +306,8 @@
             att[s, pos, pl.ds(0, 48), :] = clean[b * 48 : (b + 1) * 48]
             att[s, pos, pl.ds(48, 48), :] = noisy[b * 48 : (b + 1) * 48]
 
+    send_wp(0)
+    send_wp(1)
     last = chunk(pair(3, 1 - zl), pair(2, 1 - zl))
     own = None
     for group in ((2, 1), (3, 0)):

time: 86.9 us -> 93.9 us (1.081)
  Pallas kernels: 84.6 us -> 90.8 us
    pallas_call x1, Pallas kernels: 84.6 us -> 90.8 us  [shards(): pl.pallas_call(kernel, out_shape=jax.ShapeDtypeStruct((48, 8192), BF16),...]
    unnamed x1 -> x7, local copies, waits for them, and re-layouts: 2.06 us -> 2.91 us
where the time goes in v6:
time: 93.9 us; the launch traced here: 93.7 us
  Pallas kernels  90.8 us (97%)
  local copies, waits for them, and re-layouts  2.91 us (3%)
    pallas_call x1, Pallas kernels, shards(): pl.pallas_call(kernel, out_shape=jax.ShapeDtypeStruct((48, 8192), BF16),...  90.8 us
    unnamed x7, local copies, waits for them, and re-layouts  2.91 us

profile of v6, /device:TPU:0, one launch (start us, length us, event | category | flops | bytes accessed | tf_op | source)
XLA Modules:
  0.0 93.7 jit_solution(4625268742630633541)
XLA Ops:
  0.0 0.0 copy-start
  0.0 0.7 copy-done
  0.7 0.0 copy-start.1
  0.7 0.7 copy-done.1
  1.4 0.0 copy-start.2
  1.4 0.7 copy-done.2
  2.0 90.8 %whole.1 = bf16[48,8192]{1,0:T(8,128)(2,1)S(1)} custom-call(s32[32]{0:T(128)S(1)} %copy-done.2, bf16[384,4096]{1,0:T(8,128)(2,1)} %act.1, s32[384]{0:T(512)S(1)} %copy-done.1, bf16[4096]{0:T(1024)(128)(2,1)S(1)} %copy-done, bf16[3,4096,512]{2,1,0:T(8,128)(2,1)} %w.1, bf16[512,4096]{1,0:T(8,128)(2,1)} %wo.1), custom_call_target="tpu_custom_call" | custom-call | tf_op jit(solution)/shard_map/whole/pallas_call | solution.py:400
  92.9 0.9 copy.8
Async XLA Ops:
  0.0 0.7 copy-start
  0.7 0.7 copy-start.1
  1.4 0.7 copy-start.2

commit v7 on v3

--- a/solution.py
+++ b/solution.py
@@ -347,15 +347,15 @@
         out[:, pl.ds(col, NC)] = total[:48]
         out[:, pl.ds(4096 + col, NC)] = total[48:]
 
-    for n in range(4):
+    for n in range(8):
         matmul(n)
     for n in range(16):
         reduce_x(n)
-        if n + 4 < 16:
-            matmul(n + 4)
-        if n >= 3:
-            reduce_z(n - 3)
-    for n in (13, 14, 15):
+        if n + 8 < 16:
+            matmul(n + 8)
+        if n >= 6:
+            reduce_z(n - 6)
+    for n in range(10, 16):
         reduce_z(n)
     for cp in sends:
         cp.wait_send()

time: 85.3 us -> 83.1 us (0.974)
  Pallas kernels: 83 us -> 80.8 us
    pallas_call x1, Pallas kernels: 83 us -> 80.8 us  [shards(): pl.pallas_call(kernel, out_shape=jax.ShapeDtypeStruct((48, 8192), BF16),...]
where the time goes in v7:
time: 83.1 us; the launch traced here: 82.9 us
  Pallas kernels  80.8 us (97%)
  local copies, waits for them, and re-layouts  2.06 us (2%)
    pallas_call x1, Pallas kernels, shards(): pl.pallas_call(kernel, out_shape=jax.ShapeDtypeStruct((48, 8192), BF16),...  80.8 us
    unnamed x1, local copies, waits for them, and re-layouts  2.06 us

profile of v7, /device:TPU:0, one launch (start us, length us, event | category | flops | bytes accessed | tf_op | source)
XLA Modules:
  0.0 82.9 jit_solution(2005567524135539245)
XLA Ops:
  0.0 80.8 %whole.1 = bf16[48,8192]{1,0:T(8,128)(2,1)} custom-call(s32[32]{0:T(128)} %span.1, bf16[384,4096]{1,0:T(8,128)(2,1)} %act.1, s32[384]{0:T(512)} %nmask.1, bf16[4096]{0:T(1024)(128)(2,1)} %mvec.1, bf16[3,4096,512]{2,1,0:T(8,128)(2,1)} %w.1, bf16[512,4096]{1,0:T(8,128)(2,1)} %wo.1), custom_call_target="tpu_custom_call" | custom-call | tf_op jit(solution)/shard_map/whole/pallas_call | solution.py:374
  80.9 2.1 %copy.8 = bf16[48,8192]{1,0:T(8,128)(2,1)} copy(bf16[48,8192]{1,0:T(8,128)(2,1)} %whole.1) | data formatting | bytes 1572864

commit v8 on v5

--- a/solution.py
+++ b/solution.py
@@ -139,6 +139,10 @@
             start(rcopy(st.at[m, ys[k], rows], dst, f_s.at[m - 1, k], f_r.at[m - 1, me], ydev[k]))
         kv[me, m - 1] = st[m, y, rows]
     start(rcopy(kv.at[me], kv.at[me], c_s.at[0], g_r.at[me], cdev))
+    for m in (1, 2):
+        dst = kv.at[me, m - 1]
+        start(rcopy(st.at[m, ys[2], rows], dst, f_s.at[m - 1, 2], f_r.at[m - 1, me], ydev[2]))
+        start(rcopy(st.at[m, ys[2], rows], dst, f_s.at[m - 1, 0], f_r.at[m - 1, me], ddev))
     def here(k, z, split):
         slot = ctx_of(ys[k], z, c)
         if split:
@@ -245,10 +249,6 @@
         slot = here(k, zl, True)
         to_z(n, slot)
         to_core(2 + n, slot)
-    for m in (1, 2):
-        dst = kv.at[me, m - 1]
-        start(rcopy(st.at[m, ys[2], rows], dst, f_s.at[m - 1, 2], f_r.at[m - 1, me], ydev[2]))
-        start(rcopy(st.at[m, ys[2], rows], dst, f_s.at[m - 1, 0], f_r.at[m - 1, me], ddev))
     for k in (1, 3, 2):
         rcopy(q.at[ys[k]], q.at[ys[k]], q_s.at[1], q_r.at[ys[k]], cdev).wait_recv()
         rcopy(msk.at[ys[k]], msk.at[ys[k]], m_s.at[1], m_r.at[ys[k]], cdev).wait_recv()
@@ -371,15 +371,15 @@
         out[:, pl.ds(col, NC)] = total[:48]
         out[:, pl.ds(4096 + col, NC)] = total[48:]
 
-    for n in range(4):
+    for n in range(8):
         matmul(n)
     for n in range(16):
         reduce_x(n)
-        if n + 4 < 16:
-            matmul(n + 4)
-        if n >= 3:
-            reduce_z(n - 3)
-    for n in (13, 14, 15):
+        if n + 8 < 16:
+            matmul(n + 8)
+        if n >= 6:
+            reduce_z(n - 6)
+    for n in range(10, 16):
         reduce_z(n)
     for cp in sends:
         cp.wait_send()

time: 86.9 us -> 84.6 us (0.974)
  Pallas kernels: 84.6 us -> 82.3 us
    pallas_call x1, Pallas kernels: 84.6 us -> 82.3 us  [shards(): pl.pallas_call(kernel, out_shape=jax.ShapeDtypeStruct((48, 8192), BF16),...]
where the time goes in v8:
time: 84.6 us; the launch traced here: 84.4 us
  Pallas kernels  82.3 us (97%)
  local copies, waits for them, and re-layouts  2.06 us (2%)
    pallas_call x1, Pallas kernels, shards(): pl.pallas_call(kernel, out_shape=jax.ShapeDtypeStruct((48, 8192), BF16),...  82.3 us
    unnamed x1, local copies, waits for them, and re-layouts  2.06 us

profile of v8, /device:TPU:0, one launch (start us, length us, event | category | flops | bytes accessed | tf_op | source)
XLA Modules:
  0.0 84.4 jit_solution(8886672032299858092)
XLA Ops:
  0.0 82.3 %whole.1 = bf16[48,8192]{1,0:T(8,128)(2,1)} custom-call(s32[32]{0:T(128)} %span.1, bf16[384,4096]{1,0:T(8,128)(2,1)} %act.1, s32[384]{0:T(512)} %nmask.1, bf16[4096]{0:T(1024)(128)(2,1)} %mvec.1, bf16[3,4096,512]{2,1,0:T(8,128)(2,1)} %w.1, bf16[512,4096]{1,0:T(8,128)(2,1)} %wo.1), custom_call_target="tpu_custom_call" | custom-call | tf_op jit(solution)/shard_map/whole/pallas_call | solution.py:398
  82.3 2.1 %copy.8 = bf16[48,8192]{1,0:T(8,128)(2,1)} copy(bf16[48,8192]{1,0:T(8,128)(2,1)} %whole.1) | data formatting | bytes 1572864
